TPU v7x, 512 devices: a whole 4x4x16 slice. The times are simulated.
512 devices in a mesh: tm: 16 (over y, x), space: 32 (over z, core).
Axes of the slice: x: 4, y: 4, z: 16, core: 2. Of those that a mesh axis runs over, the one named last changes fastest.
Arguments:
- lagrange: float32 [16, 4, 1024, 256], P('tm', None, 'space'), may hold values from -6 to 6
- obs_mult: float32 [16, 2, 4, 1024, 256], P('tm', None, None, 'space'), may hold values from -6 to 6
- increment: float32 [16, 4, 1024, 256], P('tm', None, 'space'), may hold values from -6 to 6
- model_side: float32 [16, 4, 1024, 256], P('tm', None, 'space'), may hold values from -6 to 6
- obs_side: float32 [16, 2, 4, 1024, 256], P('tm', None, None, 'space'), may hold values from -6 to 6
- model_var: float32 [16, 4, 1024, 256], P('tm', None, 'space'), may hold values from 0.5 to 2
- obs_var: float32 [16, 2, 4, 1024, 256], P('tm', None, None, 'space'), may hold values from 0.5 to 2
- courant_x: float32 [4, 1024, 256], P(None, 'space'), may hold values from -0.5 to 0.5
- courant_y: float32 [4, 1024, 256], P(None, 'space'), may hold values from -0.5 to 0.5
- diffusion: float32 [4, 1024, 256], P(None, 'space'), may hold values from 0.08 to 0.22
Outputs:
- lagrange_next: float32 [16, 4, 1024, 256], P('tm', None, 'space')
- obs_mult_next: float32 [16, 2, 4, 1024, 256], P('tm', None, None, 'space')
- increment_next: float32 [16, 4, 1024, 256], P('tm', None, 'space')
All inputs are finite; a program needn't handle non-finite values.
Results may differ from a plain program's by a relative error of at most 0.000028.
Values sent between devices are 32-bit elements; how exact they have to be, the bound alone decides.
No kernel may reach another device: no remote copies, remote signals or barrier semaphores. Data moves between devices by JAX's collectives and lax.ppermute only.
A program may use at most 64 MiB of HBM per device.

v0:
```python
import jax
import jax.numpy as jnp
from jax import lax
from jax.sharding import PartitionSpec as P

STEPS = 4


def padded(array, sides, width):
    for axis, dim in sides:
        size, length = (lax.axis_size(axis), array.shape[dim])
        up = [(i, (i + 1) % size) for i in range(size)]
        down = [(j, i) for i, j in up]
        last = lax.slice_in_dim(array, length - width, length, axis=dim)
        first = lax.slice_in_dim(array, 0, width, axis=dim)
        before = lax.ppermute(last, axis, up)
        after = lax.ppermute(first, axis, down)
        array = jnp.concatenate([before, array, after], axis=dim)
    return array


def from_behind(block, axis, distance):
    devices = range(lax.axis_size(axis))
    route = [(i - distance, i) for i in devices if i - distance in devices]
    return lax.ppermute(block, axis, route)


def carried_in(value, axis, join, neutral, backward):
    count, mine = (lax.axis_size(axis), lax.axis_index(axis))
    pieces = lax.all_gather(value, axis)
    if backward:
        pieces = pieces[::-1]
        mine = count - 1 - mine
    total = jnp.full_like(value, 0) + jnp.asarray(neutral, value.dtype)

    def step(position, total):
        longer = join(total, pieces[position])
        return jnp.where(position < mine, longer, total)

    return lax.fori_loop(0, count - 1, step, total)


def shift_north(field):
    return jnp.concatenate([field[..., 1:], jnp.zeros_like(field[..., :1])], axis=-1)


def shift_south(field):
    return jnp.concatenate([jnp.zeros_like(field[..., :1]), field[..., :-1]], axis=-1)


def tangent_step(extended, coefs):
    central = extended[:, 1:-1]
    inner = coefs[:, :, 1:-1]
    eastern = extended[:, 2:]
    western = extended[:, :-2]
    northern = shift_north(central)
    southern = shift_south(central)
    return (
        central
        - 0.5 * inner[0] * (eastern - western)
        - 0.5 * inner[1] * (northern - southern)
        + inner[2] * (eastern + western + northern + southern - 4.0 * central)
    )


def adjoint_step(extended, coefs):
    flux_x = coefs[0] * extended
    flux_y = coefs[1][:, 1:-1] * extended[:, 1:-1]
    spread = coefs[2] * extended
    central = spread[:, 1:-1]
    return (
        extended[:, 1:-1]
        + 0.5 * (flux_x[:, 2:] - flux_x[:, :-2])
        + 0.5 * (shift_north(flux_y) - shift_south(flux_y))
        + spread[:, 2:]
        + spread[:, :-2]
        + shift_north(central)
        + shift_south(central)
        - 4.0 * central
    )


def tangent_run(start, coef_ext, rim_width):
    extended = start
    margin = 0
    middle = start
    for step_index in range(STEPS):
        extended = padded(extended, (("space", 1),), rim_width)
        margin = rim_width
        extended = tangent_step(extended, coef_ext)
        margin = margin - 1
        if step_index == STEPS // 2 - 1:
            middle = extended
    return (middle, extended)


def adjoint_run(start, forcing, coef_ext, rim_width):
    extended = start
    margin = 0
    for step_index in range(STEPS):
        if step_index == STEPS // 2:
            extended = extended + forcing
        extended = padded(extended, (("space", 1),), rim_width)
        margin = rim_width
        extended = adjoint_step(extended, coef_ext)
        margin = margin - 1
    return extended


def add_fields(earlier, later):
    return earlier + later


def body(
    lagrange,
    obs_mult,
    increment,
    model_side,
    obs_side,
    model_var,
    obs_var,
    courant_x,
    courant_y,
    diffusion,
):
    coef_width = 1
    state_width = 1
    adjoint_width = 1
    coefs = jnp.stack([courant_x, courant_y, diffusion])
    coef_ext = padded(coefs, (("space", 2),), coef_width)
    middle_state, final_state = tangent_run(increment[0], coef_ext, state_width)
    previous = from_behind(final_state, "tm", 1)
    resid_model = model_side[0] - model_var[0] * lagrange[0] - (increment[0] - previous)
    observed = jnp.stack([middle_state, final_state])
    resid_obs = obs_side[0] - obs_var[0] * obs_mult[0] - observed
    following = from_behind(lagrange[0], "tm", -1)
    pulled = adjoint_run(obs_mult[0, 1] - following, obs_mult[0, 0], coef_ext, adjoint_width)
    resid_state = -(lagrange[0] + pulled)
    earlier = carried_in(resid_model, "tm", add_fields, jnp.zeros_like(resid_model), False)
    later = carried_in(resid_state, "tm", add_fields, jnp.zeros_like(resid_state), True)
    z_model = earlier + resid_model
    z_state = later + resid_state
    z_obs = resid_obs / obs_var[0]
    cross_local = (
        jnp.sum(resid_model * z_model) + jnp.sum(resid_obs * z_obs) + jnp.sum(resid_state * z_state)
    )
    square_local = jnp.sum(z_model * z_model) + jnp.sum(z_obs * z_obs) + jnp.sum(z_state * z_state)
    cross_sum, square_sum = lax.psum((cross_local, square_local), ("tm", "space"))
    step_len = cross_sum / (square_sum + 1e-06)
    lagrange_next = (lagrange[0] + step_len * z_model)[None]
    obs_mult_next = (obs_mult[0] + step_len * z_obs)[None]
    increment_next = (increment[0] + step_len * z_state)[None]
    return (lagrange_next, obs_mult_next, increment_next)


def solution(mesh):
    placed = (
        P("tm", None, "space", None),
        P("tm", None, None, "space", None),
        P("tm", None, "space", None),
        P("tm", None, "space", None),
        P("tm", None, None, "space", None),
        P("tm", None, "space", None),
        P("tm", None, None, "space", None),
        P(None, "space", None),
        P(None, "space", None),
        P(None, "space", None),
    )
    return jax.shard_map(
        body,
        mesh=mesh,
        in_specs=placed,
        out_specs=(
            P("tm", None, "space", None),
            P("tm", None, None, "space", None),
            P("tm", None, "space", None),
        ),
        check_vma=False,
    )
```

profile of v0, /device:TPU:1, one launch (start us, length us, event | category | flops | bytes accessed | tf_op | source)
XLA Modules:
  0.0 306.8 jit_solution(14007687805331886875)
XLA Ops:
  7.2 0.9 fusion.62
  8.1 6.9 %collective-permute-start = (f32[4,1,256]{2,1,0:T(1,128)S(1)}, f32[4,1,256]{2,1,0:T(1,128)S(1)}, u32[]{:S(2)}, u32[]{:S(2)}) collective-permute-start(f32[4,1,256]{2,1,0:T(1,128)S(1)} %get-tuple-element.276), channel_id=1, source_target_pairs={{1,0},{2,1},{3,2},{4,3},{5,4},{6,5},{7,6},{8,7},{9,8},{10,9},{11,1... | collective-permute-start | bytes 12296 | tf_op jit(solution)/shard_map/ppermute | solution.py:17
  15.0 0.9 pad_maximum_fusion.15
  15.9 3.6 %collective-permute-start.11 = (f32[3,4,1,256]{3,2,1,0:T(1,128)S(1)}, f32[3,4,1,256]{3,2,1,0:T(1,128)S(1)}, u32[]{:S(2)}, u32[]{:S(2)}) collective-permute-start(f32[3,4,1,256]{3,2,1,0:T(1,128)S(1)} %get-tuple-element.236), channel_id=1, source_target_pairs={{1,0},{2,1},{3,2},{4,3},{5,4},{6,5},{7,6},{8,7},{9,8},{10,9},{11,1... | collective-permute-start | bytes 36872 | tf_op jit(solution)/shard_map/ppermute | solution.py:17
  19.5 1.3 collective-permute-start.9
  20.8 1.1 fusion.63
  21.9 1.3 multiply_add_fusion.3
  23.2 3.0 collective-permute-start.2
  26.3 0.7 collective-permute-done.2
  27.0 0.3 collective-permute-done.3
  27.4 0.1 multiply_add_fusion.2
  27.5 3.6 %collective-permute-start.4 = (f32[4,1,256]{2,1,0:T(1,128)S(1)}, f32[4,1,256]{2,1,0:T(1,128)S(1)}, u32[]{:S(2)}, u32[]{:S(2)}) collective-permute-start(f32[4,1,256]{2,1,0:T(1,128)S(1)} %get-tuple-element.268), channel_id=1, source_target_pairs={{1,0},{2,1},{3,2},{4,3},{5,4},{6,5},{7,6},{8,7},{9,8},{10,9},{11,1... | collective-permute-start | bytes 12296 | tf_op jit(solution)/shard_map/ppermute | solution.py:17
  31.2 0.7 collective-permute-done.4
  31.9 0.3 collective-permute-done.5
  32.3 0.1 multiply_add_fusion.1
  32.5 3.1 %collective-permute-start.6 = (f32[4,1,256]{2,1,0:T(1,128)S(1)}, f32[4,1,256]{2,1,0:T(1,128)S(1)}, u32[]{:S(2)}, u32[]{:S(2)}) collective-permute-start(f32[4,1,256]{2,1,0:T(1,128)S(1)} %get-tuple-element.264), channel_id=1, source_target_pairs={{1,0},{2,1},{3,2},{4,3},{5,4},{6,5},{7,6},{8,7},{9,8},{10,9},{11,1... | collective-permute-start | bytes 12296 | tf_op jit(solution)/shard_map/ppermute | solution.py:17
  35.7 0.7 collective-permute-done.6
  36.4 0.3 collective-permute-done.7
  36.8 0.1 multiply_add_fusion
  36.9 4.0 %collective-permute-start.8 = (f32[4,32,256]{2,1,0:T(8,128)S(1)}, f32[4,32,256]{2,1,0:T(8,128)S(1)}, u32[]{:S(2)}, u32[]{:S(2)}) collective-permute-start(f32[4,32,256]{2,1,0:T(8,128)S(1)} %multiply_add_fusion), channel_id=1, source_target_pairs={{0,32},{32,64},{64,96},{96,128},{128,160},{160,192},{192,224},{224... | collective-permute-start | bytes 393224 | tf_op jit(solution)/shard_map/ppermute | solution.py:25
  41.0 2.2 collective-permute-start.12
  43.1 1.3 collective-permute-start.13
  44.5 0.5 collective-permute-done.12
  45.0 1.1 collective-permute-done.13
  46.3 0.2 slice_multiply_fusion.6
  46.5 2.5 collective-permute-start.15
  49.1 0.5 collective-permute-done.14
  49.7 0.2 collective-permute-done.15
  50.0 0.2 slice_multiply_fusion.5
  50.2 3.4 %collective-permute-start.17 = (f32[4,1,256]{2,1,0:T(1,128)S(1)}, f32[4,1,256]{2,1,0:T(1,128)S(1)}, u32[]{:S(2)}, u32[]{:S(2)}) collective-permute-start(f32[4,1,256]{2,1,0:T(1,128)S(1)} %get-tuple-element.254), channel_id=1, source_target_pairs={{1,0},{2,1},{3,2},{4,3},{5,4},{6,5},{7,6},{8,7},{9,8},{10,9},{11,1... | collective-permute-start | bytes 12296 | tf_op jit(solution)/shard_map/ppermute | solution.py:17
  53.7 0.5 collective-permute-done.16
  54.3 0.2 collective-permute-done.17
  54.7 0.2 slice_multiply_fusion.4
  54.9 3.4 %collective-permute-start.19 = (f32[4,1,256]{2,1,0:T(1,128)S(1)}, f32[4,1,256]{2,1,0:T(1,128)S(1)}, u32[]{:S(2)}, u32[]{:S(2)}) collective-permute-start(f32[4,1,256]{2,1,0:T(1,128)S(1)} %get-tuple-element.250), channel_id=1, source_target_pairs={{1,0},{2,1},{3,2},{4,3},{5,4},{6,5},{7,6},{8,7},{9,8},{10,9},{11,1... | collective-permute-start | bytes 12296 | tf_op jit(solution)/shard_map/ppermute | solution.py:17
  58.4 0.5 collective-permute-done.18
  58.9 0.2 collective-permute-done.19
  59.3 0.8 fusion.14
  60.2 0.7 all-gather.7.cloned.1.call-update
  61.0 0.8 multiply_reduce_fusion
  61.8 59.2 %all-gather.5.cloned.1.call-done = f32[64,32,256]{2,1,0:T(8,128)} async-done(((f32[4,32,256]{2,1,0:T(8,128)}), f32[64,32,256]{2,1,0:T(8,128)}) %all-gather.5.cloned.1.call-update) | async-done | bytes 2097168 | tf_op jit(solution)/shard_map/all_gather | solution.py:30
  121.0 14.6 %while.28 = (s32[]{:T(128)}, f32[4,32,256]{2,1,0:T(8,128)S(1)}, s32[]{:T(128)}, f32[16,4,32,256]{3,2,1,0:T(8,128)}, s32[]{:T(128)}, /*index=5*/s32[]{:T(128)}) while((s32[]{:T(128)}, f32[4,32,256]{2,1,0:T(8,128)S(1)}, s32[]{:T(128)}, f32[16,4,32,256]{3,2,1,0:T(8,128)}, s32[]{:T(128)}, /*index=5*/s32[]{:T(128)}) %tuple.109), condition=%wide.region_1.2_spmd.clone, body=%wide.region_0.1_spmd.clone.sunk | while | flops 98308 | bytes 393309 | solution.py:40
  121.0 0.9 add_select_fusion.4
  121.9 1.0 add_select_fusion.4
  122.9 1.0 add_select_fusion.4
  123.9 1.0 add_select_fusion.4
  124.9 1.0 add_select_fusion.4
  125.8 1.0 add_select_fusion.4
  126.8 1.0 add_select_fusion.4
  127.8 1.0 add_select_fusion.4
  128.8 1.0 add_select_fusion.4
  129.7 1.0 add_select_fusion.4
  130.7 1.0 add_select_fusion.4
  131.7 1.0 add_select_fusion.4
  132.7 1.0 add_select_fusion.4
  133.6 1.0 add_select_fusion.4
  134.6 1.0 add_select_fusion.4
  135.6 1.3 multiply_reduce_fusion.3
  136.9 47.4 %all-gather.7.cloned.1.call-done = f32[64,32,256]{2,1,0:T(8,128)} async-done(((f32[4,32,256]{2,1,0:T(8,128)}), f32[64,32,256]{2,1,0:T(8,128)}) %all-gather.7.cloned.1.call-update) | async-done | bytes 2097168 | tf_op jit(solution)/shard_map/all_gather | solution.py:30
  184.3 1.7 rev.3
  186.0 1.1 while.29
  187.1 0.6 multiply_reduce_fusion.2
  191.6 104.6 %all-reduce.24 = (f32[]{:T(128)}, f32[]{:T(128)}) all-reduce(f32[]{:T(128)S(6)} %add.310, f32[]{:T(128)S(6)} %add.312), channel_id=1, replica_groups=mesh['tm'=16,'space'=32] {'tm','space'}, use_global_device_ids=true, to_apply=%region_7.8 | all-reduce | flops 2 | bytes 16 | tf_op jit(solution)/shard_map/psum | solution.py:148
  297.4 0.8 fusion.2
  298.2 1.7 add_bitcast_fusion
  (83 shorter events, 2.3 us)
Async XLA Ops:
  7.2 20.2 %copy-start.2 = (f32[4,32,256]{2,1,0:T(8,128)S(1)}, f32[4,32,256]{2,1,0:T(8,128)}, u32[]{:S(2)}) copy-start(f32[4,32,256]{2,1,0:T(8,128)} %param.21) | copy-start | bytes 393220
  7.2 20.2 %copy-start.1 = (f32[4,32,256]{2,1,0:T(8,128)S(1)}, f32[4,32,256]{2,1,0:T(8,128)}, u32[]{:S(2)}) copy-start(f32[4,32,256]{2,1,0:T(8,128)} %param.22) | copy-start | bytes 393220
  7.2 20.2 %copy-start = (f32[4,32,256]{2,1,0:T(8,128)S(1)}, f32[4,32,256]{2,1,0:T(8,128)}, u32[]{:S(2)}) copy-start(f32[4,32,256]{2,1,0:T(8,128)} %param.23) | copy-start | bytes 393220
  7.2 113.8 %all-gather.5.cloned.1.call-start = ((), (), s32[]{:S(2)}) async-start(), calls=%async_computation | async-start | bytes 2228224 | tf_op jit(solution)/shard_map/all_gather | solution.py:30
  8.1 13.7 %collective-permute-start = (f32[4,1,256]{2,1,0:T(1,128)S(1)}, f32[4,1,256]{2,1,0:T(1,128)S(1)}, u32[]{:S(2)}, u32[]{:S(2)}) collective-permute-start(f32[4,1,256]{2,1,0:T(1,128)S(1)} %get-tuple-element.276), channel_id=1, source_target_pairs={{1,0},{2,1},{3,2},{4,3},{5,4},{6,5},{7,6},{8,7},{9,8},{10,9},{11,1... | collective-permute-start | bytes 12296 | tf_op jit(solution)/shard_map/ppermute | solution.py:17
  15.0 6.8 %collective-permute-start.1 = (f32[4,1,256]{2,1,0:T(1,128)S(1)}, f32[4,1,256]{2,1,0:T(1,128)S(1)}, u32[]{:S(2)}, u32[]{:S(2)}) collective-permute-start(f32[4,1,256]{2,1,0:T(1,128)S(1)} %get-tuple-element.275), channel_id=1, source_target_pairs={{0,1},{1,2},{2,3},{3,4},{4,5},{5,6},{6,7},{7,8},{8,9},{9,10},{10,1... | collective-permute-start | bytes 12296 | tf_op jit(solution)/shard_map/ppermute | solution.py:16
  15.9 19.7 %collective-permute-start.10 = (f32[3,4,1,256]{3,2,1,0:T(1,128)S(1)}, f32[3,4,1,256]{3,2,1,0:T(1,128)S(1)}, u32[]{:S(2)}, u32[]{:S(2)}) collective-permute-start(f32[3,4,1,256]{3,2,1,0:T(1,128)S(1)} %get-tuple-element.235), channel_id=1, source_target_pairs={{0,1},{1,2},{2,3},{3,4},{4,5},{5,6},{6,7},{7,8},{8,9},{9,10},{10,1... | collective-permute-start | bytes 36872 | tf_op jit(solution)/shard_map/ppermute | solution.py:16
  15.9 19.7 %collective-permute-start.11 = (f32[3,4,1,256]{3,2,1,0:T(1,128)S(1)}, f32[3,4,1,256]{3,2,1,0:T(1,128)S(1)}, u32[]{:S(2)}, u32[]{:S(2)}) collective-permute-start(f32[3,4,1,256]{3,2,1,0:T(1,128)S(1)} %get-tuple-element.236), channel_id=1, source_target_pairs={{1,0},{2,1},{3,2},{4,3},{5,4},{6,5},{7,6},{8,7},{9,8},{10,9},{11,1... | collective-permute-start | bytes 36872 | tf_op jit(solution)/shard_map/ppermute | solution.py:17
  19.5 21.4 %collective-permute-start.9 = (f32[4,32,256]{2,1,0:T(8,128)}, f32[4,32,256]{2,1,0:T(8,128)S(1)}, u32[]{:S(2)}, u32[]{:S(2)}) collective-permute-start(f32[4,32,256]{2,1,0:T(8,128)} %bitcast.105), channel_id=1, source_target_pairs={{32,0},{64,32},{96,64},{128,96},{160,128},{192,160},{224,192},{256... | collective-permute-start | bytes 393224 | tf_op jit(solution)/shard_map/ppermute | solution.py:25
  23.2 3.8 %collective-permute-start.2 = (f32[4,1,256]{2,1,0:T(1,128)S(1)}, f32[4,1,256]{2,1,0:T(1,128)S(1)}, u32[]{:S(2)}, u32[]{:S(2)}) collective-permute-start(f32[4,1,256]{2,1,0:T(1,128)S(1)} %get-tuple-element.272), channel_id=1, source_target_pairs={{1,0},{2,1},{3,2},{4,3},{5,4},{6,5},{7,6},{8,7},{9,8},{10,9},{11,1... | collective-permute-start | bytes 12296 | tf_op jit(solution)/shard_map/ppermute | solution.py:17
  26.2 1.2 collective-permute-start.3
  27.5 13.4 %copy-start.4 = (f32[1,2,4,32,256]{4,3,2,1,0:T(8,128)S(1)}, f32[1,2,4,32,256]{4,3,2,1,0:T(8,128)}, u32[]{:S(2)}) copy-start(f32[1,2,4,32,256]{4,3,2,1,0:T(8,128)} %param.15) | copy-start | bytes 786436
  27.5 4.4 %collective-permute-start.4 = (f32[4,1,256]{2,1,0:T(1,128)S(1)}, f32[4,1,256]{2,1,0:T(1,128)S(1)}, u32[]{:S(2)}, u32[]{:S(2)}) collective-permute-start(f32[4,1,256]{2,1,0:T(1,128)S(1)} %get-tuple-element.268), channel_id=1, source_target_pairs={{1,0},{2,1},{3,2},{4,3},{5,4},{6,5},{7,6},{8,7},{9,8},{10,9},{11,1... | collective-permute-start | bytes 12296 | tf_op jit(solution)/shard_map/ppermute | solution.py:17
  31.1 1.2 collective-permute-start.5
  32.5 3.9 %collective-permute-start.6 = (f32[4,1,256]{2,1,0:T(1,128)S(1)}, f32[4,1,256]{2,1,0:T(1,128)S(1)}, u32[]{:S(2)}, u32[]{:S(2)}) collective-permute-start(f32[4,1,256]{2,1,0:T(1,128)S(1)} %get-tuple-element.264), channel_id=1, source_target_pairs={{1,0},{2,1},{3,2},{4,3},{5,4},{6,5},{7,6},{8,7},{9,8},{10,9},{11,1... | collective-permute-start | bytes 12296 | tf_op jit(solution)/shard_map/ppermute | solution.py:17
  35.6 1.2 collective-permute-start.7
  36.9 22.4 %collective-permute-start.8 = (f32[4,32,256]{2,1,0:T(8,128)S(1)}, f32[4,32,256]{2,1,0:T(8,128)S(1)}, u32[]{:S(2)}, u32[]{:S(2)}) collective-permute-start(f32[4,32,256]{2,1,0:T(8,128)S(1)} %multiply_add_fusion), channel_id=1, source_target_pairs={{0,32},{32,64},{64,96},{96,128},{128,160},{160,192},{192,224},{224... | collective-permute-start | bytes 393224 | tf_op jit(solution)/shard_map/ppermute | solution.py:25
  41.0 4.1 %collective-permute-start.12 = (f32[4,1,256]{2,1,0:T(1,128)S(1)}, f32[4,1,256]{2,1,0:T(1,128)S(1)}, u32[]{:S(2)}, u32[]{:S(2)}) collective-permute-start(f32[4,1,256]{2,1,0:T(1,128)S(1)} %get-tuple-element.261), channel_id=1, source_target_pairs={{0,1},{1,2},{2,3},{3,4},{4,5},{5,6},{6,7},{7,8},{8,9},{9,10},{10,1... | collective-permute-start | bytes 12296 | tf_op jit(solution)/shard_map/ppermute | solution.py:16
  43.1 3.0 collective-permute-start.13
  46.5 3.2 %collective-permute-start.14 = (f32[4,1,256]{2,1,0:T(1,128)S(1)}, f32[4,1,256]{2,1,0:T(1,128)S(1)}, u32[]{:S(2)}, u32[]{:S(2)}) collective-permute-start(f32[4,1,256]{2,1,0:T(1,128)S(1)} %get-tuple-element.257), channel_id=1, source_target_pairs={{0,1},{1,2},{2,3},{3,4},{4,5},{5,6},{6,7},{7,8},{8,9},{9,10},{10,1... | collective-permute-start | bytes 12296 | tf_op jit(solution)/shard_map/ppermute | solution.py:16
  46.5 3.3 %collective-permute-start.15 = (f32[4,1,256]{2,1,0:T(1,128)S(1)}, f32[4,1,256]{2,1,0:T(1,128)S(1)}, u32[]{:S(2)}, u32[]{:S(2)}) collective-permute-start(f32[4,1,256]{2,1,0:T(1,128)S(1)} %get-tuple-element.258), channel_id=1, source_target_pairs={{1,0},{2,1},{3,2},{4,3},{5,4},{6,5},{7,6},{8,7},{9,8},{10,9},{11,1... | collective-permute-start | bytes 12296 | tf_op jit(solution)/shard_map/ppermute | solution.py:17
  50.2 4.1 %collective-permute-start.16 = (f32[4,1,256]{2,1,0:T(1,128)S(1)}, f32[4,1,256]{2,1,0:T(1,128)S(1)}, u32[]{:S(2)}, u32[]{:S(2)}) collective-permute-start(f32[4,1,256]{2,1,0:T(1,128)S(1)} %get-tuple-element.253), channel_id=1, source_target_pairs={{0,1},{1,2},{2,3},{3,4},{4,5},{5,6},{6,7},{7,8},{8,9},{9,10},{10,1... | collective-permute-start | bytes 12296 | tf_op jit(solution)/shard_map/ppermute | solution.py:16
  50.2 4.3 %collective-permute-start.17 = (f32[4,1,256]{2,1,0:T(1,128)S(1)}, f32[4,1,256]{2,1,0:T(1,128)S(1)}, u32[]{:S(2)}, u32[]{:S(2)}) collective-permute-start(f32[4,1,256]{2,1,0:T(1,128)S(1)} %get-tuple-element.254), channel_id=1, source_target_pairs={{1,0},{2,1},{3,2},{4,3},{5,4},{6,5},{7,6},{8,7},{9,8},{10,9},{11,1... | collective-permute-start | bytes 12296 | tf_op jit(solution)/shard_map/ppermute | solution.py:17
  54.5 4.8 %copy-start.3 = (f32[1,4,32,256]{3,2,1,0:T(8,128)S(1)}, f32[1,4,32,256]{3,2,1,0:T(8,128)}, u32[]{:S(2)}) copy-start(f32[1,4,32,256]{3,2,1,0:T(8,128)} %param.16) | copy-start | bytes 393220
  54.5 4.8 %copy-start.9 = (f32[1,4,32,256]{3,2,1,0:T(8,128)S(1)}, f32[1,4,32,256]{3,2,1,0:T(8,128)}, u32[]{:S(2)}) copy-start(f32[1,4,32,256]{3,2,1,0:T(8,128)} %param.14) | copy-start | bytes 393220
  54.5 4.8 %copy-start.10 = (f32[1,4,32,256]{3,2,1,0:T(8,128)S(1)}, f32[1,4,32,256]{3,2,1,0:T(8,128)}, u32[]{:S(2)}) copy-start(f32[1,4,32,256]{3,2,1,0:T(8,128)} %param.19) | copy-start | bytes 393220
  54.6 4.8 %copy-start.11 = (f32[1,4,32,256]{3,2,1,0:T(8,128)S(1)}, f32[1,4,32,256]{3,2,1,0:T(8,128)}, u32[]{:S(2)}) copy-start(f32[1,4,32,256]{3,2,1,0:T(8,128)} %param.17) | copy-start | bytes 393220
  54.8 4.1 %collective-permute-start.18 = (f32[4,1,256]{2,1,0:T(1,128)S(1)}, f32[4,1,256]{2,1,0:T(1,128)S(1)}, u32[]{:S(2)}, u32[]{:S(2)}) collective-permute-start(f32[4,1,256]{2,1,0:T(1,128)S(1)} %get-tuple-element.249), channel_id=1, source_target_pairs={{0,1},{1,2},{2,3},{3,4},{4,5},{5,6},{6,7},{7,8},{8,9},{9,10},{10,1... | collective-permute-start | bytes 12296 | tf_op jit(solution)/shard_map/ppermute | solution.py:16
  54.9 4.3 %collective-permute-start.19 = (f32[4,1,256]{2,1,0:T(1,128)S(1)}, f32[4,1,256]{2,1,0:T(1,128)S(1)}, u32[]{:S(2)}, u32[]{:S(2)}) collective-permute-start(f32[4,1,256]{2,1,0:T(1,128)S(1)} %get-tuple-element.250), channel_id=1, source_target_pairs={{1,0},{2,1},{3,2},{4,3},{5,4},{6,5},{7,6},{8,7},{9,8},{10,9},{11,1... | collective-permute-start | bytes 12296 | tf_op jit(solution)/shard_map/ppermute | solution.py:17
  58.3 2.7 copy-start.7
  58.3 2.7 copy-start.8
  60.2 75.4 %copy-start.6 = (f32[4,32,256]{2,1,0:T(8,128)S(1)}, f32[4,32,256]{2,1,0:T(8,128)}, u32[]{:S(2)}) copy-start(f32[4,32,256]{2,1,0:T(8,128)} %get-tuple-element.246) | copy-start | bytes 393220
  60.2 124.1 %all-gather.7.cloned.1.call-start = ((), (), s32[]{:S(2)}) async-start(), calls=%async_computation.1 | async-start | bytes 2228224 | tf_op jit(solution)/shard_map/all_gather | solution.py:30
  186.0 1.1 copy-start.5
Sparse Core Ops, SparseCore 0:
  60.3 60.5 all-gather.4
  124.5 59.6 all-gather.6
where the time goes:
time: 307 us
  waiting for transfers between devices  114 us (37%)
  blocking collectives  105 us (34%)
  starting transfers between devices  38.4 us (13%)
  other arithmetic  24.3 us (8%)
  between operations  19.6 us (6%)
  local copies, waits for them, and re-layouts  4.85 us (2%)
    all_gather x2, waiting for transfers between devices, carried_in(): pieces = lax.all_gather(value, axis)  107 us
    psum x1, blocking collectives, body(): lax.psum((cross_local, square_local), ('tm', 'space'))  105 us
    ppermute x9, starting transfers between devices, padded(): after = lax.ppermute(first, axis, down)  30.7 us
    select_n x30, other arithmetic, step(): return jnp.where(position < mine, longer, total)  14.9 us
  transfers between devices with their start and end apart: 22, of which 16 were waited for; matrix products, arithmetic and copies ran while one was open for 7% of the time, Pallas kernels for 0%

commit v1 on v0

v1 whole, which is shorter than its diff:
```python
import functools

import jax
import jax.numpy as jnp
from jax import lax
from jax.experimental import pallas as pl
from jax.experimental.pallas import tpu as pltpu
from jax.sharding import PartitionSpec as P

STEPS = 4
LEV = 4
ROWS = 32
NY = 256
NW = 16
HALF = 128
EDGE = 7
F32 = jnp.float32

VMEM = pl.BlockSpec(memory_space=pltpu.VMEM)
ANY = pl.BlockSpec(memory_space=pl.ANY)


def call(kernel, out_shape, in_specs, out_specs, scratch=(), **kw):
    return pl.pallas_call(
        kernel,
        out_shape=out_shape,
        in_specs=in_specs,
        out_specs=out_specs,
        scratch_shapes=list(scratch),
        compiler_params=pltpu.CompilerParams(vmem_limit_bytes=16 * 1024 * 1024),
        **kw,
    )


def lower_half(shape):
    return lax.broadcasted_iota(jnp.int32, shape, 0) < 4


def pack_kernel(inc, obs, lag, cx, cy, df, first_out, last_out, first, last, sem):
    sources = [inc.at[0], obs.at[0, 1], obs.at[0, 0], lag.at[0], cx, cy, df]
    copies = []
    for f, src in enumerate(sources):
        copies.append(pltpu.make_async_copy(src.at[:, pl.ds(0, 8)], first.at[f], sem.at[2 * f]))
        copies.append(pltpu.make_async_copy(src.at[:, pl.ds(ROWS - 8, 8)], last.at[f], sem.at[2 * f + 1]))
    for c in copies:
        c.start()
    for c in copies:
        c.wait()
    low = lower_half((8, NY))
    for f in range(EDGE):
        for m in range(2):
            k = 8 * (2 * f + m)
            first_out[k : k + 8, :] = jnp.where(low, first[f, 2 * m], pltpu.roll(first[f, 2 * m + 1], 4, 0))
            last_out[k : k + 8, :] = jnp.where(low, pltpu.roll(last[f, 2 * m], 4, 0), last[f, 2 * m + 1])


def halo(nxt, prv, f, l):
    k = 8 * (2 * f + l // 2)
    low = lower_half((8, NY))
    a, b = nxt[k : k + 8, :], prv[k : k + 8, :]
    if l % 2 == 0:
        return jnp.where(low, a, pltpu.roll(b, 4, 0))
    return jnp.where(low, pltpu.roll(a, 4, 0), b)


def extend(core, nxt, prv, f, l):
    return jnp.concatenate([core, halo(nxt, prv, f, l)], axis=0)


def east(x):
    return pltpu.roll(x, ROWS + 7, 0)


def west(x):
    return pltpu.roll(x, 1, 0)


def north(x):
    return pltpu.roll(x, NY - 1, 1)


def south(x):
    return pltpu.roll(x, 1, 1)


def tangent(q, c):
    a0, ae, aw, an, as_ = c
    return a0 * q + ae * east(q) + aw * west(q) + an * north(q) + as_ * south(q)


def adjoint(p, c):
    a0, ae, aw, an, as_ = c
    return a0 * p + east(aw * p) + west(ae * p) + north(as_ * p) + south(an * p)


def run_kernel(inc, obs, lag, cx, cy, df, mside, mvar, oside, ovar, nxt, prv, send, zobs, part):
    col = lax.broadcasted_iota(jnp.int32, (ROWS + 8, NY), 1)
    cross = jnp.zeros((ROWS, NY), F32)
    square = jnp.zeros((ROWS, NY), F32)
    for l in range(LEV):
        ext = lambda core, f: extend(core, nxt, prv, f, l)
        x, y, d = ext(cx[l], 4), ext(cy[l], 5), ext(df[l], 6)
        x, y = 0.5 * x, 0.5 * y
        coefs = (
            1.0 - 4.0 * d,
            d - x,
            d + x,
            jnp.where(col == NY - 1, 0.0, d - y),
            jnp.where(col == 0, 0.0, d + y),
        )
        q = ext(inc[0, l], 0)
        for step in range(STEPS):
            q = tangent(q, coefs)
            if step == STEPS // 2 - 1:
                middle = q[:ROWS]
        final = q[:ROWS]
        p = ext(obs[0, 1, l], 1)
        b = ext(lag[0, l], 3)
        for step in range(STEPS):
            if step == STEPS // 2:
                p = p + ext(obs[0, 0, l], 2)
            p = adjoint(p, coefs)
            b = adjoint(b, coefs)
        lagr = lag[0, l]
        fixed = mside[0, l] - mvar[0, l] * lagr - inc[0, l]
        with_lag = lagr + p[:ROWS]
        b = b[:ROWS]
        for k in range(4):
            rows = slice(8 * k, 8 * k + 8)
            t = 4 * l + k
            send[t, 0:8, :] = fixed[rows]
            send[t, 8:16, :] = final[rows]
            send[t, 16:24, :] = with_lag[rows]
            send[t, 24:32, :] = b[rows]
        for j, state in enumerate((middle, final)):
            var = ovar[0, j, l]
            resid = oside[0, j, l] - var * obs[0, j, l] - state
            z = resid / var
            zobs[j, l] = z
            cross = cross + resid * z
            square = square + z * z
    fold = lambda v: v[0:8] + v[8:16] + v[16:24] + v[24:32]
    part[0] = fold(cross)
    part[1] = fold(square)


def sum_kernel(recv, part, back):
    cross, square = part[0], part[1]
    z = jnp.zeros((8, NY), F32)
    before = jnp.zeros((8, NY), F32)
    for w in range(NW):
        r = recv[w, 0:8, :] + before
        before = recv[w, 8:16, :]
        z = z + r
        cross = cross + r * z
        square = square + z * z
        back[w, 0:8, :] = z[:, :HALF]
        back[w, 8:16, :] = z[:, HALF:]
    z = jnp.zeros((8, NY), F32)
    after = jnp.zeros((8, NY), F32)
    for w in reversed(range(NW)):
        r = after - recv[w, 16:24, :]
        after = recv[w, 24:32, :]
        z = z + r
        cross = cross + r * z
        square = square + z * z
        back[w, 16:24, :] = z[:, :HALF]
        back[w, 24:32, :] = z[:, HALF:]

    def fold(v):
        v = v[:, :HALF] + v[:, HALF:]
        return v + pltpu.roll(v, HALF // 2, 1)

    lane = lax.broadcasted_iota(jnp.int32, (8, HALF), 1)
    both = jnp.where(lane < HALF // 2, fold(cross), fold(square))
    for w in range(NW):
        back[w, 32:40, :] = both


def scalar_kernel(count, recv, out):
    total = recv[0]
    for w in range(1, NW):
        total = total + recv[w]
    row = jnp.sum(total, axis=0, keepdims=True)
    for s in range(count):
        out[s] = row


def update_kernel(count, sums, recv, lag, obs, inc, zobs, lag_out, obs_out, inc_out):
    total = sums[0]
    for s in range(1, count):
        total = total + sums[s]
    lane = lax.broadcasted_iota(jnp.int32, (1, HALF), 1)
    cross = jnp.sum(jnp.where(lane < HALF // 2, total, 0.0), axis=1, keepdims=True)
    square = jnp.sum(jnp.where(lane < HALF // 2, 0.0, total), axis=1, keepdims=True)
    step = cross / (square + 1e-06)
    for l in range(LEV):
        for k in range(4):
            rows = slice(8 * k, 8 * k + 8)
            t = 4 * l + k
            for h in range(2):
                cols = slice(HALF * h, HALF * h + HALF)
                lag_out[0, l, rows, cols] = lag[0, l, rows, cols] + step * recv[t, 8 * h : 8 * h + 8, :]
                inc_out[0, l, rows, cols] = inc[0, l, rows, cols] + step * recv[t, 16 + 8 * h : 24 + 8 * h, :]
        for j in range(2):
            obs_out[0, j, l] = obs[0, j, l] + step * zobs[j, l]


def body(lag, obs, inc, mside, oside, mvar, ovar, cx, cy, df):
    sds = jax.ShapeDtypeStruct
    size = lax.axis_size("space")
    edge = sds((EDGE * LEV * 4, NY), F32)
    first, last = call(
        pack_kernel,
        (edge, edge),
        [ANY] * 6,
        (VMEM, VMEM),
        [
            pltpu.VMEM((EDGE, LEV, 8, NY), F32),
            pltpu.VMEM((EDGE, LEV, 8, NY), F32),
            pltpu.SemaphoreType.DMA((2 * EDGE,)),
        ],
        name="pack_edges",
    )(inc, obs, lag, cx, cy, df)
    nxt = lax.ppermute(first, "space", [((i + 1) % size, i) for i in range(size)])
    prv = lax.ppermute(last, "space", [(i, (i + 1) % size) for i in range(size)])
    send, zobs, part = call(
        run_kernel,
        (sds((NW, 32, NY), F32), sds((2, LEV, ROWS, NY), F32), sds((2, 8, NY), F32)),
        [VMEM] * 12,
        (VMEM, VMEM, VMEM),
        name="stencil_runs",
    )(inc, obs, lag, cx, cy, df, mside, mvar, oside, ovar, nxt, prv)
    recv = lax.all_to_all(send, "tm", 0, 0)
    back = call(sum_kernel, sds((NW, 40, HALF), F32), [VMEM] * 2, VMEM, name="window_sums")(recv, part)
    back = lax.all_to_all(back, "tm", 0, 0)
    sums = call(
        functools.partial(scalar_kernel, size),
        sds((size, 1, HALF), F32),
        [pl.BlockSpec((NW, 8, HALF), lambda i: (0, 4, 0))],
        pl.BlockSpec((size, 1, HALF), lambda i: (0, 0, 0)),
        grid=(1,),
        name="scalars",
    )(back)
    sums = lax.all_to_all(sums, "space", 0, 0)
    return call(
        functools.partial(update_kernel, size),
        (sds(lag.shape, F32), sds(obs.shape, F32), sds(inc.shape, F32)),
        [VMEM] * 6,
        (VMEM, VMEM, VMEM),
        name="update",
    )(sums, back, lag, obs, inc, zobs)


def solution(mesh):
    field = P("tm", None, "space", None)
    pair = P("tm", None, None, "space", None)
    coef = P(None, "space", None)
    return jax.shard_map(
        body,
        mesh=mesh,
        in_specs=(field, pair, field, field, pair, field, pair, coef, coef, coef),
        out_specs=(field, pair, field),
        check_vma=False,
    )
```

time: 307 us -> 73.6 us (0.24)
  waiting for transfers between devices: 114 us -> 4.37 us
  blocking collectives: 105 us -> 52.2 us
  starting transfers between devices: 38.4 us -> 6.89 us
  other arithmetic: 24.3 us -> 0 us
  between operations: 19.6 us -> 0.69 us
  Pallas kernels: 0 us -> 3.6 us
    all_gather x2 -> x0, waiting for transfers between devices: 107 us -> none  [carried_in(): pieces = lax.all_gather(value, axis)]
    psum x1 -> x0, blocking collectives: 105 us -> none  [body(): lax.psum((cross_local, square_local), ('tm', 'space'))]
    all_to_all x0 -> x3, blocking collectives: none -> 52.2 us  [the longest x1 26 us: body(): sums = lax.all_to_all(sums, 'space', 0, 0)]
    ppermute x20 -> x2, starting transfers between devices: 38.3 us -> 6.89 us  [the longest x1 6.89 us: body(): lax.ppermute(first, 'space', [((i + 1) % size, i) for i in range(size)])]
    select_n x30 -> x0, other arithmetic: 14.9 us -> none  [step(): return jnp.where(position < mine, longer, total)]
    unnamed x24 -> x26, local copies, waits for them, and re-layouts: 0.07 us -> 5.49 us
    pallas_call x0 -> x5, Pallas kernels: none -> 3.6 us  [the longest x1 2.17 us: body(): call(run_kernel, (sds((NW, 32, NY), F32), sds((2, LEV, ROWS, NY), F32), s...]
    ppermute x20 -> x2, waiting for transfers between devices: 7.05 us -> 4.37 us  [the longest x1 3.41 us: body(): lax.ppermute(last, 'space', [(i, (i + 1) % size) for i in range(size)])]
  transfers between devices with their start and end apart: 22 -> 2, of which waited for: 16 -> 2; matrix products, arithmetic and copies ran while one was open for 7% -> 0% of each run, Pallas kernels for 0% -> 0%
where the time goes in v1:
time: 73.6 us; the launch traced here: 73.3 us
  blocking collectives  52.2 us (71%)
  starting transfers between devices  6.89 us (9%)
  local copies, waits for them, and re-layouts  5.49 us (7%)
  waiting for transfers between devices  4.37 us (6%)
  Pallas kernels  3.6 us (5%)
    all_to_all x1, blocking collectives, body(): sums = lax.all_to_all(sums, 'space', 0, 0)  26 us
    all_to_all x1, blocking collectives, body(): recv = lax.all_to_all(send, 'tm', 0, 0)  15.5 us
    all_to_all x1, blocking collectives, body(): back = lax.all_to_all(back, 'tm', 0, 0)  10.7 us
    ppermute x1, starting transfers between devices, body(): lax.ppermute(first, 'space', [((i + 1) % size, i) for i in range(size)])  6.89 us
    unnamed x26, local copies, waits for them, and re-layouts  5.49 us
    ppermute x1, waiting for transfers between devices, body(): lax.ppermute(last, 'space', [(i, (i + 1) % size) for i in range(size)])  3.41 us
    pallas_call x1, Pallas kernels, body(): call(run_kernel, (sds((NW, 32, NY), F32), sds((2, LEV, ROWS, NY), F32), s...  2.17 us
  transfers between devices with their start and end apart: 2, of which 2 were waited for; matrix products, arithmetic and copies ran while one was open for 0% of the time, Pallas kernels for 0%

profile of v1, /device:TPU:1, one launch (start us, length us, event | category | flops | bytes accessed | tf_op | source)
XLA Modules:
  0.0 73.3 jit_solution(14456347452108428037)
XLA Ops:
  0.6 0.0 copy-start
  0.6 0.9 %copy-done = f32[1,2,4,32,256]{4,3,2,1,0:T(8,128)S(1)} copy-done((f32[1,2,4,32,256]{4,3,2,1,0:T(8,128)S(1)}, f32[1,2,4,32,256]{4,3,2,1,0:T(8,128)}, u32[]{:S(2)}) %copy-start) | copy-done | bytes 262168
  1.6 0.0 copy-start.2
  1.6 0.9 %copy-done.2 = f32[1,4,32,256]{3,2,1,0:T(8,128)S(1)} copy-done((f32[1,4,32,256]{3,2,1,0:T(8,128)S(1)}, f32[1,4,32,256]{3,2,1,0:T(8,128)}, u32[]{:S(2)}) %copy-start.2) | copy-done | bytes 131096
  2.5 0.0 copy-start.4
  2.5 0.9 %copy-done.4 = f32[1,4,32,256]{3,2,1,0:T(8,128)S(1)} copy-done((f32[1,4,32,256]{3,2,1,0:T(8,128)S(1)}, f32[1,4,32,256]{3,2,1,0:T(8,128)}, u32[]{:S(2)}) %copy-start.4) | copy-done | bytes 131096
  3.4 0.0 copy-start.6
  3.4 0.9 %copy-done.6 = f32[4,32,256]{2,1,0:T(8,128)S(1)} copy-done((f32[4,32,256]{2,1,0:T(8,128)S(1)}, f32[4,32,256]{2,1,0:T(8,128)}, u32[]{:S(2)}) %copy-start.6) | copy-done | bytes 131096
  4.3 0.0 copy-start.7
  4.3 0.9 %copy-done.7 = f32[4,32,256]{2,1,0:T(8,128)S(1)} copy-done((f32[4,32,256]{2,1,0:T(8,128)S(1)}, f32[4,32,256]{2,1,0:T(8,128)}, u32[]{:S(2)}) %copy-start.7) | copy-done | bytes 131096
  5.2 0.0 copy-start.8
  5.2 0.9 %copy-done.8 = f32[4,32,256]{2,1,0:T(8,128)S(1)} copy-done((f32[4,32,256]{2,1,0:T(8,128)S(1)}, f32[4,32,256]{2,1,0:T(8,128)}, u32[]{:S(2)}) %copy-start.8) | copy-done | bytes 131096
  6.1 0.0 copy-start.9
  6.1 0.0 copy-start.10
  6.1 0.0 copy-start.11
  6.1 0.0 copy-start.12
  6.1 0.3 pack_edges.1
  6.5 6.9 %collective-permute-start = (f32[112,256]{1,0:T(8,128)S(1)}, f32[112,256]{1,0:T(8,128)S(1)}, u32[]{:S(2)}, u32[]{:S(2)}) collective-permute-start(f32[112,256]{1,0:T(8,128)S(1)} %get-tuple-element.8), channel_id=1, source_target_pairs={{1,0},{2,1},{3,2},{4,3},{5,4},{6,5},{7,6},{8,7},{9,8},{10,9},{11,1... | collective-permute-start | bytes 344072 | tf_op jit(solution)/shard_map/ppermute | solution.py:225
  13.3 0.0 collective-permute-start.1
  13.3 1.0 %collective-permute-done.nxt = f32[112,256]{1,0:T(8,128)S(1)} collective-permute-done((f32[112,256]{1,0:T(8,128)S(1)}, f32[112,256]{1,0:T(8,128)S(1)}, u32[]{:S(2)}, u32[]{:S(2)}) %collective-permute-start) | collective-permute-done | bytes 114720 | tf_op jit(solution)/shard_map/ppermute | solution.py:225
  14.3 3.4 %collective-permute-done.1.prv = f32[112,256]{1,0:T(8,128)S(1)} collective-permute-done((f32[112,256]{1,0:T(8,128)S(1)}, f32[112,256]{1,0:T(8,128)S(1)}, u32[]{:S(2)}, u32[]{:S(2)}) %collective-permute-start.1) | collective-permute-done | bytes 114720 | tf_op jit(solution)/shard_map/ppermute | solution.py:226
  17.7 0.0 copy-done.9
  17.7 0.0 copy-done.10
  17.7 0.0 copy-done.11
  17.7 0.0 copy-done.12
  17.7 2.2 %stencil_runs.1 = (f32[16,32,256]{2,1,0:T(8,128)S(1)}, f32[2,4,32,256]{3,2,1,0:T(8,128)S(1)}, f32[2,8,256]{2,1,0:T(8,128)S(1)}) custom-call(f32[1,4,32,256]{3,2,1,0:T(8,128)S(1)} %copy-done.2, f32[1,2,4,32,256]{4,3,2,1,0:T(8,128)S(1)} %copy-done, f32[1,4,32,256]{3,2,1,0:T(8,128)S(1)} %copy-done.4, f32[4,32,256]{2,1,0:T(8,128)S(1)} %copy-done.6, ...), custom_call_target="tpu_custom_call" | custom-call | tf_op jit(solution)/shard_map/stencil_runs/pallas_call | solution.py:227
  19.9 15.5 %all_to_all.15.recv = f32[16,32,256]{2,1,0:T(8,128)S(1)} all-to-all(f32[16,32,256]{2,1,0:T(8,128)S(1)} %get-tuple-element.10), channel_id=1, replica_groups=mesh['tm'=16,'space'=32] {'tm'}, dimensions={0} | all-to-all | bytes 1048576 | tf_op jit(solution)/shard_map/all_to_all | solution.py:234
  35.5 0.1 window_sums.1
  35.6 0.0 copy-start.3
  35.6 0.0 copy-start.5
  35.6 10.7 %all_to_all.16.recv = f32[16,40,128]{2,1,0:T(8,128)S(1)} all-to-all(f32[16,40,128]{2,1,0:T(8,128)S(1)} %window_sums.1), channel_id=1, replica_groups=mesh['tm'=16,'space'=32] {'tm'}, dimensions={0} | all-to-all | bytes 655360 | tf_op jit(solution)/shard_map/all_to_all | solution.py:236
  46.3 0.0 copy-start.1
  46.3 26.0 %all_to_all.17.sums = f32[32,1,128]{2,1,0:T(1,128)S(1)} all-to-all(f32[32,1,128]{2,1,0:T(1,128)S(1)} %scalars.1), channel_id=1, replica_groups=mesh['tm'=16,'space'=32] {'space'}, dimensions={0} | all-to-all | bytes 32768 | tf_op jit(solution)/shard_map/all_to_all | solution.py:245
  72.3 0.0 copy-done.3
  72.3 0.0 copy-done.5
  72.3 0.0 copy-done.1
  72.4 0.9 %update.1 = (f32[1,4,32,256]{3,2,1,0:T(8,128)}, f32[1,2,4,32,256]{4,3,2,1,0:T(8,128)}, f32[1,4,32,256]{3,2,1,0:T(8,128)}) custom-call(f32[32,1,128]{2,1,0:T(1,128)S(1)} %all_to_all.17.sums, f32[16,40,128]{2,1,0:T(8,128)S(1)} %all_to_all.16.recv, f32[1,4,32,256]{3,2,1,0:T(8,128)S(1)} %copy-done.5, f32[1,2,4,32,256]{4,3,2,1,0:T(8,128)S(1)} %copy-done.1, ...), custom_call_target="tpu_custom_call" | custom-call | tf_op jit(solution)/shard_map/update/pallas_call | solution.py:246
  (1 shorter events, 0.0 us)
Async XLA Ops:
  0.6 1.0 %copy-start = (f32[1,2,4,32,256]{4,3,2,1,0:T(8,128)S(1)}, f32[1,2,4,32,256]{4,3,2,1,0:T(8,128)}, u32[]{:S(2)}) copy-start(f32[1,2,4,32,256]{4,3,2,1,0:T(8,128)} %obs.5) | copy-start | bytes 786436
  1.6 0.9 %copy-start.2 = (f32[1,4,32,256]{3,2,1,0:T(8,128)S(1)}, f32[1,4,32,256]{3,2,1,0:T(8,128)}, u32[]{:S(2)}) copy-start(f32[1,4,32,256]{3,2,1,0:T(8,128)} %inc.5) | copy-start | bytes 393220
  2.5 0.9 %copy-start.4 = (f32[1,4,32,256]{3,2,1,0:T(8,128)S(1)}, f32[1,4,32,256]{3,2,1,0:T(8,128)}, u32[]{:S(2)}) copy-start(f32[1,4,32,256]{3,2,1,0:T(8,128)} %lag.5) | copy-start | bytes 393220
  3.4 0.9 %copy-start.6 = (f32[4,32,256]{2,1,0:T(8,128)S(1)}, f32[4,32,256]{2,1,0:T(8,128)}, u32[]{:S(2)}) copy-start(f32[4,32,256]{2,1,0:T(8,128)} %cx.3) | copy-start | bytes 393220
  4.3 0.9 %copy-start.7 = (f32[4,32,256]{2,1,0:T(8,128)S(1)}, f32[4,32,256]{2,1,0:T(8,128)}, u32[]{:S(2)}) copy-start(f32[4,32,256]{2,1,0:T(8,128)} %cy.3) | copy-start | bytes 393220
  5.2 0.9 %copy-start.8 = (f32[4,32,256]{2,1,0:T(8,128)S(1)}, f32[4,32,256]{2,1,0:T(8,128)}, u32[]{:S(2)}) copy-start(f32[4,32,256]{2,1,0:T(8,128)} %df.3) | copy-start | bytes 393220
  6.1 11.6 %copy-start.9 = (f32[1,2,4,32,256]{4,3,2,1,0:T(8,128)S(1)}, f32[1,2,4,32,256]{4,3,2,1,0:T(8,128)}, u32[]{:S(2)}) copy-start(f32[1,2,4,32,256]{4,3,2,1,0:T(8,128)} %oside.1) | copy-start | bytes 786436
  6.1 11.6 %copy-start.10 = (f32[1,2,4,32,256]{4,3,2,1,0:T(8,128)S(1)}, f32[1,2,4,32,256]{4,3,2,1,0:T(8,128)}, u32[]{:S(2)}) copy-start(f32[1,2,4,32,256]{4,3,2,1,0:T(8,128)} %ovar.1) | copy-start | bytes 786436
  6.1 11.6 %copy-start.11 = (f32[1,4,32,256]{3,2,1,0:T(8,128)S(1)}, f32[1,4,32,256]{3,2,1,0:T(8,128)}, u32[]{:S(2)}) copy-start(f32[1,4,32,256]{3,2,1,0:T(8,128)} %mside.1) | copy-start | bytes 393220
  6.1 11.6 %copy-start.12 = (f32[1,4,32,256]{3,2,1,0:T(8,128)S(1)}, f32[1,4,32,256]{3,2,1,0:T(8,128)}, u32[]{:S(2)}) copy-start(f32[1,4,32,256]{3,2,1,0:T(8,128)} %mvar.1) | copy-start | bytes 393220
  6.5 7.9 %collective-permute-start = (f32[112,256]{1,0:T(8,128)S(1)}, f32[112,256]{1,0:T(8,128)S(1)}, u32[]{:S(2)}, u32[]{:S(2)}) collective-permute-start(f32[112,256]{1,0:T(8,128)S(1)} %get-tuple-element.8), channel_id=1, source_target_pairs={{1,0},{2,1},{3,2},{4,3},{5,4},{6,5},{7,6},{8,7},{9,8},{10,9},{11,1... | collective-permute-start | bytes 344072 | tf_op jit(solution)/shard_map/ppermute | solution.py:225
  13.3 4.4 %collective-permute-start.1 = (f32[112,256]{1,0:T(8,128)S(1)}, f32[112,256]{1,0:T(8,128)S(1)}, u32[]{:S(2)}, u32[]{:S(2)}) collective-permute-start(f32[112,256]{1,0:T(8,128)S(1)} %get-tuple-element.9), channel_id=1, source_target_pairs={{0,1},{1,2},{2,3},{3,4},{4,5},{5,6},{6,7},{7,8},{8,9},{9,10},{10,1... | collective-permute-start | bytes 344072 | tf_op jit(solution)/shard_map/ppermute | solution.py:226
  35.6 36.7 %copy-start.3 = (f32[1,4,32,256]{3,2,1,0:T(8,128)S(1)}, f32[1,4,32,256]{3,2,1,0:T(8,128)}, u32[]{:S(2)}) copy-start(f32[1,4,32,256]{3,2,1,0:T(8,128)} %inc.5) | copy-start | bytes 393220
  35.6 36.7 %copy-start.5 = (f32[1,4,32,256]{3,2,1,0:T(8,128)S(1)}, f32[1,4,32,256]{3,2,1,0:T(8,128)}, u32[]{:S(2)}) copy-start(f32[1,4,32,256]{3,2,1,0:T(8,128)} %lag.5) | copy-start | bytes 393220
  46.3 26.0 %copy-start.1 = (f32[1,2,4,32,256]{4,3,2,1,0:T(8,128)S(1)}, f32[1,2,4,32,256]{4,3,2,1,0:T(8,128)}, u32[]{:S(2)}) copy-start(f32[1,2,4,32,256]{4,3,2,1,0:T(8,128)} %obs.5) | copy-start | bytes 786436

commit v2 on v1

--- a/solution.py
+++ b/solution.py
@@ -36,15 +36,19 @@
     return lax.broadcasted_iota(jnp.int32, shape, 0) < 4
 
 
-def pack_kernel(inc, obs, lag, cx, cy, df, first_out, last_out, first, last, sem):
+def fetch_kernel(*refs):
+    args, (first_out, last_out), copies_out = refs[:10], refs[10:12], refs[12:22]
+    first, last, edge_sem, bulk_sem = refs[22:]
+    lag, obs, inc, _, _, _, _, cx, cy, df = args
     sources = [inc.at[0], obs.at[0, 1], obs.at[0, 0], lag.at[0], cx, cy, df]
-    copies = []
+    edges = []
     for f, src in enumerate(sources):
-        copies.append(pltpu.make_async_copy(src.at[:, pl.ds(0, 8)], first.at[f], sem.at[2 * f]))
-        copies.append(pltpu.make_async_copy(src.at[:, pl.ds(ROWS - 8, 8)], last.at[f], sem.at[2 * f + 1]))
-    for c in copies:
+        edges.append(pltpu.make_async_copy(src.at[:, pl.ds(0, 8)], first.at[f], edge_sem.at[2 * f]))
+        edges.append(pltpu.make_async_copy(src.at[:, pl.ds(ROWS - 8, 8)], last.at[f], edge_sem.at[2 * f + 1]))
+    bulk = [pltpu.make_async_copy(src, dst, bulk_sem.at[i]) for i, (src, dst) in enumerate(zip(args, copies_out))]
+    for c in edges + bulk:
         c.start()
-    for c in copies:
+    for c in edges:
         c.wait()
     low = lower_half((8, NY))
     for f in range(EDGE):
@@ -52,6 +56,8 @@
             k = 8 * (2 * f + m)
             first_out[k : k + 8, :] = jnp.where(low, first[f, 2 * m], pltpu.roll(first[f, 2 * m + 1], 4, 0))
             last_out[k : k + 8, :] = jnp.where(low, pltpu.roll(last[f, 2 * m], 4, 0), last[f, 2 * m + 1])
+    for c in bulk:
+        c.wait()
 
 
 def halo(nxt, prv, f, l):
@@ -210,18 +216,21 @@
     sds = jax.ShapeDtypeStruct
     size = lax.axis_size("space")
     edge = sds((EDGE * LEV * 4, NY), F32)
-    first, last = call(
-        pack_kernel,
-        (edge, edge),
-        [ANY] * 6,
-        (VMEM, VMEM),
+    args = (lag, obs, inc, mside, oside, mvar, ovar, cx, cy, df)
+    args = [pltpu.with_memory_space_constraint(x, pltpu.HBM) for x in args]
+    first, last, lag, obs, inc, mside, oside, mvar, ovar, cx, cy, df = call(
+        fetch_kernel,
+        (edge, edge) + tuple(sds(x.shape, F32) for x in args),
+        [ANY] * 10,
+        (VMEM,) * 12,
         [
             pltpu.VMEM((EDGE, LEV, 8, NY), F32),
             pltpu.VMEM((EDGE, LEV, 8, NY), F32),
             pltpu.SemaphoreType.DMA((2 * EDGE,)),
+            pltpu.SemaphoreType.DMA((10,)),
         ],
-        name="pack_edges",
-    )(inc, obs, lag, cx, cy, df)
+        name="fetch",
+    )(*args)
     nxt = lax.ppermute(first, "space", [((i + 1) % size, i) for i in range(size)])
     prv = lax.ppermute(last, "space", [(i, (i + 1) % size) for i in range(size)])
     send, zobs, part = call(

time: 73.6 us -> 69.2 us (0.940)
  local copies, waits for them, and re-layouts: 5.49 us -> 0 us
  Pallas kernels: 3.6 us -> 5.09 us
    unnamed x26 -> x0, local copies, waits for them, and re-layouts: 5.49 us -> none
    pallas_call x1, Pallas kernels: 0.32 us -> 1.82 us  [body(): call(fetch_kernel, (edge, edge) + tuple((sds(x.shape, F32) for x in args)...]
where the time goes in v2:
time: 69.2 us; the launch traced here: 69 us
  blocking collectives  52 us (75%)
  starting transfers between devices  6.89 us (10%)
  Pallas kernels  5.09 us (7%)
  waiting for transfers between devices  4.37 us (6%)
    all_to_all x1, blocking collectives, body(): sums = lax.all_to_all(sums, 'space', 0, 0)  25.9 us
    all_to_all x1, blocking collectives, body(): recv = lax.all_to_all(send, 'tm', 0, 0)  15.5 us
    all_to_all x1, blocking collectives, body(): back = lax.all_to_all(back, 'tm', 0, 0)  10.6 us
    ppermute x1, starting transfers between devices, body(): lax.ppermute(first, 'space', [((i + 1) % size, i) for i in range(size)])  6.89 us
    ppermute x1, waiting for transfers between devices, body(): lax.ppermute(last, 'space', [(i, (i + 1) % size) for i in range(size)])  3.41 us
    pallas_call x1, Pallas kernels, body(): call(run_kernel, (sds((NW, 32, NY), F32), sds((2, LEV, ROWS, NY), F32), s...  2.17 us
    pallas_call x1, Pallas kernels, body(): call(fetch_kernel, (edge, edge) + tuple((sds(x.shape, F32) for x in args)...  1.82 us
  transfers between devices with their start and end apart: 2, of which 2 were waited for; matrix products, arithmetic and copies ran while one was open for 0% of the time, Pallas kernels for 0%

profile of v2, /device:TPU:1, one launch (start us, length us, event | category | flops | bytes accessed | tf_op | source)
XLA Modules:
  0.0 69.0 jit_solution(6471479520531277074)
XLA Ops:
  0.6 1.8 %fetch.1 = (f32[112,256]{1,0:T(8,128)S(1)}, f32[112,256]{1,0:T(8,128)S(1)}, f32[1,4,32,256]{3,2,1,0:T(8,128)S(1)}, f32[1,2,4,32,256]{4,3,2,1,0:T(8,128)S(1)}, f3...) custom-call(f32[1,4,32,256]{3,2,1,0:T(8,128)} %refs_0_.1, ...), custom_call_target="tpu_custom_call" | custom-call | tf_op jit(solution)/shard_map/fetch/pallas_call | solution.py:221
  2.5 6.9 %collective-permute-start = (f32[112,256]{1,0:T(8,128)S(1)}, f32[112,256]{1,0:T(8,128)S(1)}, u32[]{:S(2)}, u32[]{:S(2)}) collective-permute-start(f32[112,256]{1,0:T(8,128)S(1)} %get-tuple-element.28), channel_id=1, source_target_pairs={{1,0},{2,1},{3,2},{4,3},{5,4},{6,5},{7,6},{8,7},{9,8},{10,9},{11,1... | collective-permute-start | bytes 344072 | tf_op jit(solution)/shard_map/ppermute | solution.py:234
  9.4 0.0 collective-permute-start.1
  9.4 1.0 %collective-permute-done.nxt = f32[112,256]{1,0:T(8,128)S(1)} collective-permute-done((f32[112,256]{1,0:T(8,128)S(1)}, f32[112,256]{1,0:T(8,128)S(1)}, u32[]{:S(2)}, u32[]{:S(2)}) %collective-permute-start) | collective-permute-done | bytes 114720 | tf_op jit(solution)/shard_map/ppermute | solution.py:234
  10.3 3.4 %collective-permute-done.1.prv = f32[112,256]{1,0:T(8,128)S(1)} collective-permute-done((f32[112,256]{1,0:T(8,128)S(1)}, f32[112,256]{1,0:T(8,128)S(1)}, u32[]{:S(2)}, u32[]{:S(2)}) %collective-permute-start.1) | collective-permute-done | bytes 114720 | tf_op jit(solution)/shard_map/ppermute | solution.py:235
  13.7 2.2 %stencil_runs.1 = (f32[16,32,256]{2,1,0:T(8,128)S(1)}, f32[2,4,32,256]{3,2,1,0:T(8,128)S(1)}, f32[2,8,256]{2,1,0:T(8,128)S(1)}) custom-call(f32[1,4,32,256]{3,2,1,0:T(8,128)S(1)} %get-tuple-element.18.inc, f32[1,2,4,32,256]{4,3,2,1,0:T(8,128)S(1)} %get-tuple-element.19.obs, f32[1,4,32,256]{3,2,1,0:T(8,128)S(1)} %get-tuple-element.20.lag, ...), custom_call_target="tpu_custom_call" | custom-call | tf_op jit(solution)/shard_map/stencil_runs/pallas_call | solution.py:236
  15.9 15.5 %all_to_all.15.recv = f32[16,32,256]{2,1,0:T(8,128)S(1)} all-to-all(f32[16,32,256]{2,1,0:T(8,128)S(1)} %get-tuple-element.30), channel_id=1, replica_groups=mesh['tm'=16,'space'=32] {'tm'}, dimensions={0} | all-to-all | bytes 1048576 | tf_op jit(solution)/shard_map/all_to_all | solution.py:243
  31.5 0.1 window_sums.1
  31.6 10.6 %all_to_all.16.recv = f32[16,40,128]{2,1,0:T(8,128)S(1)} all-to-all(f32[16,40,128]{2,1,0:T(8,128)S(1)} %window_sums.1), channel_id=1, replica_groups=mesh['tm'=16,'space'=32] {'tm'}, dimensions={0} | all-to-all | bytes 655360 | tf_op jit(solution)/shard_map/all_to_all | solution.py:245
  42.2 25.9 %all_to_all.17.sums = f32[32,1,128]{2,1,0:T(1,128)S(1)} all-to-all(f32[32,1,128]{2,1,0:T(1,128)S(1)} %scalars.1), channel_id=1, replica_groups=mesh['tm'=16,'space'=32] {'space'}, dimensions={0} | all-to-all | bytes 32768 | tf_op jit(solution)/shard_map/all_to_all | solution.py:254
  68.0 0.9 %update.1 = (f32[1,4,32,256]{3,2,1,0:T(8,128)}, f32[1,2,4,32,256]{4,3,2,1,0:T(8,128)}, f32[1,4,32,256]{3,2,1,0:T(8,128)}) custom-call(f32[32,1,128]{2,1,0:T(1,128)S(1)} %all_to_all.17.sums, f32[16,40,128]{2,1,0:T(8,128)S(1)} %all_to_all.16.recv, f32[1,4,32,256]{3,2,1,0:T(8,128)S(1)} %get-tuple-element.20.lag, ...), custom_call_target="tpu_custom_call" | custom-call | tf_op jit(solution)/shard_map/update/pallas_call | solution.py:255
  (1 shorter events, 0.0 us)
Async XLA Ops:
  2.5 7.9 %collective-permute-start = (f32[112,256]{1,0:T(8,128)S(1)}, f32[112,256]{1,0:T(8,128)S(1)}, u32[]{:S(2)}, u32[]{:S(2)}) collective-permute-start(f32[112,256]{1,0:T(8,128)S(1)} %get-tuple-element.28), channel_id=1, source_target_pairs={{1,0},{2,1},{3,2},{4,3},{5,4},{6,5},{7,6},{8,7},{9,8},{10,9},{11,1... | collective-permute-start | bytes 344072 | tf_op jit(solution)/shard_map/ppermute | solution.py:234
  9.4 4.4 %collective-permute-start.1 = (f32[112,256]{1,0:T(8,128)S(1)}, f32[112,256]{1,0:T(8,128)S(1)}, u32[]{:S(2)}, u32[]{:S(2)}) collective-permute-start(f32[112,256]{1,0:T(8,128)S(1)} %get-tuple-element.29), channel_id=1, source_target_pairs={{0,1},{1,2},{2,3},{3,4},{4,5},{5,6},{6,7},{7,8},{8,9},{9,10},{10,1... | collective-permute-start | bytes 344072 | tf_op jit(solution)/shard_map/ppermute | solution.py:235

commit v3 on v1

--- a/solution.py
+++ b/solution.py
@@ -36,7 +36,7 @@
     return lax.broadcasted_iota(jnp.int32, shape, 0) < 4
 
 
-def pack_kernel(inc, obs, lag, cx, cy, df, first_out, last_out, first, last, sem):
+def edge_kernel(lag, obs, inc, cx, cy, df, first_out, last_out, first, last, sem):
     sources = [inc.at[0], obs.at[0, 1], obs.at[0, 0], lag.at[0], cx, cy, df]
     copies = []
     for f, src in enumerate(sources):
@@ -63,12 +63,8 @@
     return jnp.where(low, pltpu.roll(a, 4, 0), b)
 
 
-def extend(core, nxt, prv, f, l):
-    return jnp.concatenate([core, halo(nxt, prv, f, l)], axis=0)
-
-
 def east(x):
-    return pltpu.roll(x, ROWS + 7, 0)
+    return pltpu.roll(x, x.shape[0] - 1, 0)
 
 
 def west(x):
@@ -93,55 +89,67 @@
     return a0 * p + east(aw * p) + west(ae * p) + north(as_ * p) + south(an * p)
 
 
-def run_kernel(inc, obs, lag, cx, cy, df, mside, mvar, oside, ovar, nxt, prv, send, zobs, part):
-    col = lax.broadcasted_iota(jnp.int32, (ROWS + 8, NY), 1)
-    cross = jnp.zeros((ROWS, NY), F32)
-    square = jnp.zeros((ROWS, NY), F32)
+def runs(inc, obs1, obs0, lag, x, y, d):
+    col = lax.broadcasted_iota(jnp.int32, d.shape, 1)
+    x, y = 0.5 * x, 0.5 * y
+    coefs = (
+        1.0 - 4.0 * d,
+        d - x,
+        d + x,
+        jnp.where(col == NY - 1, 0.0, d - y),
+        jnp.where(col == 0, 0.0, d + y),
+    )
+    q, p, b = inc, obs1, lag
+    for step in range(STEPS):
+        if step == STEPS // 2:
+            middle = q
+            p = p + obs0
+        q = tangent(q, coefs)
+        p = adjoint(p, coefs)
+        b = adjoint(b, coefs)
+    return middle, q, p, b
+
+
+def inner_kernel(lag, obs, inc, mside, oside, mvar, ovar, cx, cy, df, fixed, states, resid, inverse):
     for l in range(LEV):
-        ext = lambda core, f: extend(core, nxt, prv, f, l)
-        x, y, d = ext(cx[l], 4), ext(cy[l], 5), ext(df[l], 6)
-        x, y = 0.5 * x, 0.5 * y
-        coefs = (
-            1.0 - 4.0 * d,
-            d - x,
-            d + x,
-            jnp.where(col == NY - 1, 0.0, d - y),
-            jnp.where(col == 0, 0.0, d + y),
-        )
-        q = ext(inc[0, l], 0)
-        for step in range(STEPS):
-            q = tangent(q, coefs)
-            if step == STEPS // 2 - 1:
-                middle = q[:ROWS]
-        final = q[:ROWS]
-        p = ext(obs[0, 1, l], 1)
-        b = ext(lag[0, l], 3)
-        for step in range(STEPS):
-            if step == STEPS // 2:
-                p = p + ext(obs[0, 0, l], 2)
-            p = adjoint(p, coefs)
-            b = adjoint(b, coefs)
         lagr = lag[0, l]
-        fixed = mside[0, l] - mvar[0, l] * lagr - inc[0, l]
-        with_lag = lagr + p[:ROWS]
-        b = b[:ROWS]
+        out = runs(inc[0, l], obs[0, 1, l], obs[0, 0, l], lagr, cx[l], cy[l], df[l])
+        for i in range(4):
+            states[i, l] = out[i] + lagr if i == 2 else out[i]
+        fixed[l] = mside[0, l] - mvar[0, l] * lagr - inc[0, l]
+        for j in range(2):
+            var = ovar[0, j, l]
+            resid[j, l] = oside[0, j, l] - var * obs[0, j, l]
+            inverse[j, l] = 1.0 / var
+
+
+def outer_kernel(first, last, nxt, prv, fixed, states, resid, inverse, send, zobs, part):
+    low = lower_half((8, NY))
+    cross = jnp.zeros((8, NY), F32)
+    square = jnp.zeros((8, NY), F32)
+    for l in range(LEV):
+        ring = [jnp.concatenate([last[f, l], halo(nxt, prv, f, l), first[f, l]], axis=0) for f in range(EDGE)]
+        out = list(runs(*ring))
+        out[2] = out[2] + ring[3]
         for k in range(4):
             rows = slice(8 * k, 8 * k + 8)
+            tiles = [states[i, l, rows, :] for i in range(4)]
+            if k == 0:
+                tiles = [jnp.where(low, o[16:24], v) for o, v in zip(out, tiles)]
+            if k == 3:
+                tiles = [jnp.where(low, v, o[0:8]) for o, v in zip(out, tiles)]
             t = 4 * l + k
-            send[t, 0:8, :] = fixed[rows]
-            send[t, 8:16, :] = final[rows]
-            send[t, 16:24, :] = with_lag[rows]
-            send[t, 24:32, :] = b[rows]
-        for j, state in enumerate((middle, final)):
-            var = ovar[0, j, l]
-            resid = oside[0, j, l] - var * obs[0, j, l] - state
-            z = resid / var
-            zobs[j, l] = z
-            cross = cross + resid * z
-            square = square + z * z
-    fold = lambda v: v[0:8] + v[8:16] + v[16:24] + v[24:32]
-    part[0] = fold(cross)
-    part[1] = fold(square)
+            send[t, 0:8, :] = fixed[l, rows, :]
+            for i in range(1, 4):
+                send[t, 8 * i : 8 * i + 8, :] = tiles[i]
+            for j in range(2):
+                r = resid[j, l, rows, :] - tiles[j]
+                z = r * inverse[j, l, rows, :]
+                zobs[j, l, rows, :] = z
+                cross = cross + r * z
+                square = square + z * z
+    part[0] = cross
+    part[1] = square
 
 
 def sum_kernel(recv, part, back):
@@ -210,27 +218,34 @@
     sds = jax.ShapeDtypeStruct
     size = lax.axis_size("space")
     edge = sds((EDGE * LEV * 4, NY), F32)
-    first, last = call(
-        pack_kernel,
-        (edge, edge),
+    tiles = sds((EDGE, LEV, 8, NY), F32)
+    one, two, four = (sds(n + (LEV, ROWS, NY), F32) for n in ((), (2,), (4,)))
+    held = [pltpu.with_memory_space_constraint(x, pltpu.HBM) for x in (lag, obs, inc, mside, oside, mvar, ovar, cx, cy, df)]
+    first, last, first_tiles, last_tiles = call(
+        edge_kernel,
+        (edge, edge, tiles, tiles),
         [ANY] * 6,
-        (VMEM, VMEM),
-        [
-            pltpu.VMEM((EDGE, LEV, 8, NY), F32),
-            pltpu.VMEM((EDGE, LEV, 8, NY), F32),
-            pltpu.SemaphoreType.DMA((2 * EDGE,)),
-        ],
-        name="pack_edges",
-    )(inc, obs, lag, cx, cy, df)
+        (VMEM,) * 4,
+        [pltpu.SemaphoreType.DMA((2 * EDGE,))],
+        name="edges",
+    )(*held[:3], *held[7:])
     nxt = lax.ppermute(first, "space", [((i + 1) % size, i) for i in range(size)])
     prv = lax.ppermute(last, "space", [(i, (i + 1) % size) for i in range(size)])
+    inner = call(
+        inner_kernel,
+        (one, four, two, two),
+        [VMEM] * 10,
+        (VMEM,) * 4,
+        name="inner_runs",
+        cost_estimate=pl.CostEstimate(flops=8 * 1024 * 1024, bytes_accessed=4 * 1024 * 1024, transcendentals=0),
+    )(*held)
     send, zobs, part = call(
-        run_kernel,
-        (sds((NW, 32, NY), F32), sds((2, LEV, ROWS, NY), F32), sds((2, 8, NY), F32)),
-        [VMEM] * 12,
+        outer_kernel,
+        (sds((NW, 32, NY), F32), two, sds((2, 8, NY), F32)),
+        [VMEM] * 8,
         (VMEM, VMEM, VMEM),
-        name="stencil_runs",
-    )(inc, obs, lag, cx, cy, df, mside, mvar, oside, ovar, nxt, prv)
+        name="outer_runs",
+    )(first_tiles, last_tiles, nxt, prv, *inner)
     recv = lax.all_to_all(send, "tm", 0, 0)
     back = call(sum_kernel, sds((NW, 40, HALF), F32), [VMEM] * 2, VMEM, name="window_sums")(recv, part)
     back = lax.all_to_all(back, "tm", 0, 0)

time: 73.6 us -> 68.1 us (0.925)
  local copies, waits for them, and re-layouts: 5.49 us -> 0.01 us
  waiting for transfers between devices: 4.37 us -> 1.6 us
  Pallas kernels: 3.6 us -> 6.01 us
    unnamed x26 -> x6, local copies, waits for them, and re-layouts: 5.49 us -> 0.01 us
    pallas_call x2 -> x3, Pallas kernels: 2.49 us -> 4.9 us  [the longest x1 2.76 us: body(): call(inner_kernel, (one, four, two, two), [VMEM] * 10, (VMEM,) * 4, name=...]
    ppermute x1, waiting for transfers between devices: 3.41 us -> 1.6 us  [body(): lax.ppermute(last, 'space', [(i, (i + 1) % size) for i in range(size)])]
    ppermute x1, waiting for transfers between devices: 0.96 us -> 0.01 us  [body(): lax.ppermute(first, 'space', [((i + 1) % size, i) for i in range(size)])]
  transfers between devices with their start and end apart: 2 -> 2, of which waited for: 2 -> 1; matrix products, arithmetic and copies ran while one was open for 0% -> 0% of each run, Pallas kernels for 0% -> 4%
where the time goes in v3:
time: 68.1 us; the launch traced here: 67.7 us
  blocking collectives  52.5 us (77%)
  starting transfers between devices  6.89 us (10%)
  Pallas kernels  6.01 us (9%)
  waiting for transfers between devices  1.6 us (2%)
    all_to_all x1, blocking collectives, body(): sums = lax.all_to_all(sums, 'space', 0, 0)  26.3 us
    all_to_all x1, blocking collectives, body(): recv = lax.all_to_all(send, 'tm', 0, 0)  15.5 us
    all_to_all x1, blocking collectives, body(): back = lax.all_to_all(back, 'tm', 0, 0)  10.7 us
    ppermute x1, starting transfers between devices, body(): lax.ppermute(first, 'space', [((i + 1) % size, i) for i in range(size)])  6.89 us
    pallas_call x1, Pallas kernels, body(): call(inner_kernel, (one, four, two, two), [VMEM] * 10, (VMEM,) * 4, name=...  2.76 us
    ppermute x1, waiting for transfers between devices, body(): lax.ppermute(last, 'space', [(i, (i + 1) % size) for i in range(size)])  1.6 us
  transfers between devices with their start and end apart: 2, of which 1 were waited for; matrix products, arithmetic and copies ran while one was open for 0% of the time, Pallas kernels for 4%

profile of v3, /device:TPU:1, one launch (start us, length us, event | category | flops | bytes accessed | tf_op | source)
XLA Modules:
  0.0 67.7 jit_solution(7825104086121096125)
XLA Ops:
  0.6 1.1 %edges.1 = (f32[112,256]{1,0:T(8,128)S(1)}, f32[112,256]{1,0:T(8,128)S(1)}, f32[7,4,8,256]{3,2,1,0:T(8,128)S(1)}, f32[7,4,8,256]{3,2,1,0:T(8,128)S(1)}) custom-call(f32[1,4,32,256]{3,2,1,0:T(8,128)} %lag.5, f32[1,2,4,32,256]{4,3,2,1,0:T(8,128)} %obs.5, f32[1,4,32,256]{3,2,1,0:T(8,128)} %inc.5, f32[4,32,256]{2,1,0:T(8,128)} %cx.3, f32[4,32,256]{2,1,0:T(8,128)} %cy.3, ...), custom_call_target="tpu_custom_call" | custom-call | tf_op jit(solution)/shard_map/edges/pallas_call | solution.py:224
  1.8 6.9 %collective-permute-start = (f32[112,256]{1,0:T(8,128)S(1)}, f32[112,256]{1,0:T(8,128)S(1)}, u32[]{:S(2)}, u32[]{:S(2)}) collective-permute-start(f32[112,256]{1,0:T(8,128)S(1)} %get-tuple-element.16), channel_id=1, source_target_pairs={{1,0},{2,1},{3,2},{4,3},{5,4},{6,5},{7,6},{8,7},{9,8},{10,9},{11,1... | collective-permute-start | bytes 344072 | tf_op jit(solution)/shard_map/ppermute | solution.py:232
  8.7 0.0 collective-permute-start.1
  8.7 2.8 %inner_runs.1 = (f32[4,32,256]{2,1,0:T(8,128)S(1)}, f32[4,4,32,256]{3,2,1,0:T(8,128)S(1)}, f32[2,4,32,256]{3,2,1,0:T(8,128)S(1)}, f32[2,4,32,256]{3,2,1,0:T(8,128)S(1)}) custom-call(f32[1,4,32,256]{3,2,1,0:T(8,128)} %lag.5, f32[1,2,4,32,256]{4,3,2,1,0:T(8,128)} %obs.5, f32[1,4,32,256]{3,2,1,0:T(8,128)} %inc.5, f32[1,4,32,256]{3,2,1,0:T(8,128)} %mside.1, ...), custom_call_target="tpu_custom_call" | custom-call | flops 8388608 | bytes 4194304 | tf_op jit(solution)/shard_map/inner_runs/pallas_call | solution.py:234
  11.4 0.0 collective-permute-done.nxt
  11.4 1.6 %collective-permute-done.1.prv = f32[112,256]{1,0:T(8,128)S(1)} collective-permute-done((f32[112,256]{1,0:T(8,128)S(1)}, f32[112,256]{1,0:T(8,128)S(1)}, u32[]{:S(2)}, u32[]{:S(2)}) %collective-permute-start.1) | collective-permute-done | bytes 114720 | tf_op jit(solution)/shard_map/ppermute | solution.py:233
  13.0 1.0 %outer_runs.1 = (f32[16,32,256]{2,1,0:T(8,128)S(1)}, f32[2,4,32,256]{3,2,1,0:T(8,128)S(1)}, f32[2,8,256]{2,1,0:T(8,128)S(1)}) custom-call(f32[7,4,8,256]{3,2,1,0:T(8,128)S(1)} %get-tuple-element.14.first, f32[7,4,8,256]{3,2,1,0:T(8,128)S(1)} %get-tuple-element.15.last, f32[112,256]{1,0:T(8,128)S(1)} %collective-permute-done.nxt, ...), custom_call_target="tpu_custom_call" | custom-call | tf_op jit(solution)/shard_map/outer_runs/pallas_call | solution.py:242
  14.1 15.5 %all_to_all.15.recv = f32[16,32,256]{2,1,0:T(8,128)S(1)} all-to-all(f32[16,32,256]{2,1,0:T(8,128)S(1)} %get-tuple-element.22), channel_id=1, replica_groups=mesh['tm'=16,'space'=32] {'tm'}, dimensions={0} | all-to-all | bytes 1048576 | tf_op jit(solution)/shard_map/all_to_all | solution.py:249
  29.6 0.1 window_sums.1
  29.7 0.0 copy-start.1
  29.7 0.0 copy-start.2
  29.8 10.7 %all_to_all.16.recv = f32[16,40,128]{2,1,0:T(8,128)S(1)} all-to-all(f32[16,40,128]{2,1,0:T(8,128)S(1)} %window_sums.1), channel_id=1, replica_groups=mesh['tm'=16,'space'=32] {'tm'}, dimensions={0} | all-to-all | bytes 655360 | tf_op jit(solution)/shard_map/all_to_all | solution.py:251
  40.4 0.0 copy-start
  40.5 26.3 %all_to_all.17.sums = f32[32,1,128]{2,1,0:T(1,128)S(1)} all-to-all(f32[32,1,128]{2,1,0:T(1,128)S(1)} %scalars.1), channel_id=1, replica_groups=mesh['tm'=16,'space'=32] {'space'}, dimensions={0} | all-to-all | bytes 32768 | tf_op jit(solution)/shard_map/all_to_all | solution.py:260
  66.8 0.0 copy-done.1
  66.8 0.0 copy-done.2
  66.8 0.0 copy-done
  66.8 0.9 %update.1 = (f32[1,4,32,256]{3,2,1,0:T(8,128)}, f32[1,2,4,32,256]{4,3,2,1,0:T(8,128)}, f32[1,4,32,256]{3,2,1,0:T(8,128)}) custom-call(f32[32,1,128]{2,1,0:T(1,128)S(1)} %all_to_all.17.sums, f32[16,40,128]{2,1,0:T(8,128)S(1)} %all_to_all.16.recv, f32[1,4,32,256]{3,2,1,0:T(8,128)S(1)} %copy-done.1, f32[1,2,4,32,256]{4,3,2,1,0:T(8,128)S(1)} %copy-done, ...), custom_call_target="tpu_custom_call" | custom-call | tf_op jit(solution)/shard_map/update/pallas_call | solution.py:261
  (1 shorter events, 0.0 us)
Async XLA Ops:
  1.8 9.7 %collective-permute-start = (f32[112,256]{1,0:T(8,128)S(1)}, f32[112,256]{1,0:T(8,128)S(1)}, u32[]{:S(2)}, u32[]{:S(2)}) collective-permute-start(f32[112,256]{1,0:T(8,128)S(1)} %get-tuple-element.16), channel_id=1, source_target_pairs={{1,0},{2,1},{3,2},{4,3},{5,4},{6,5},{7,6},{8,7},{9,8},{10,9},{11,1... | collective-permute-start | bytes 344072 | tf_op jit(solution)/shard_map/ppermute | solution.py:232
  8.7 4.4 %collective-permute-start.1 = (f32[112,256]{1,0:T(8,128)S(1)}, f32[112,256]{1,0:T(8,128)S(1)}, u32[]{:S(2)}, u32[]{:S(2)}) collective-permute-start(f32[112,256]{1,0:T(8,128)S(1)} %get-tuple-element.17), channel_id=1, source_target_pairs={{0,1},{1,2},{2,3},{3,4},{4,5},{5,6},{6,7},{7,8},{8,9},{9,10},{10,1... | collective-permute-start | bytes 344072 | tf_op jit(solution)/shard_map/ppermute | solution.py:233
  29.7 37.0 %copy-start.1 = (f32[1,4,32,256]{3,2,1,0:T(8,128)S(1)}, f32[1,4,32,256]{3,2,1,0:T(8,128)}, u32[]{:S(2)}) copy-start(f32[1,4,32,256]{3,2,1,0:T(8,128)} %lag.5) | copy-start | bytes 393220
  29.7 37.0 %copy-start.2 = (f32[1,4,32,256]{3,2,1,0:T(8,128)S(1)}, f32[1,4,32,256]{3,2,1,0:T(8,128)}, u32[]{:S(2)}) copy-start(f32[1,4,32,256]{3,2,1,0:T(8,128)} %inc.5) | copy-start | bytes 393220
  40.4 26.3 %copy-start = (f32[1,2,4,32,256]{4,3,2,1,0:T(8,128)S(1)}, f32[1,2,4,32,256]{4,3,2,1,0:T(8,128)}, u32[]{:S(2)}) copy-start(f32[1,2,4,32,256]{4,3,2,1,0:T(8,128)} %obs.5) | copy-start | bytes 786436

commit v4 on v3

--- a/solution.py
+++ b/solution.py
@@ -152,7 +152,7 @@
     part[1] = square
 
 
-def sum_kernel(recv, part, back):
+def sum_kernel(count, recv, part, back, out):
     cross, square = part[0], part[1]
     z = jnp.zeros((8, NY), F32)
     before = jnp.zeros((8, NY), F32)
@@ -181,23 +181,25 @@
 
     lane = lax.broadcasted_iota(jnp.int32, (8, HALF), 1)
     both = jnp.where(lane < HALF // 2, fold(cross), fold(square))
-    for w in range(NW):
-        back[w, 32:40, :] = both
-
-
-def scalar_kernel(count, recv, out):
-    total = recv[0]
-    for w in range(1, NW):
-        total = total + recv[w]
-    row = jnp.sum(total, axis=0, keepdims=True)
+    row = jnp.sum(both, axis=0, keepdims=True)
     for s in range(count):
         out[s] = row
 
 
-def update_kernel(count, sums, recv, lag, obs, inc, zobs, lag_out, obs_out, inc_out):
+def join_kernel(count, sums, back, out):
     total = sums[0]
     for s in range(1, count):
         total = total + sums[s]
+    tile = jnp.broadcast_to(total, (8, HALF))
+    for w in range(NW):
+        out[w, 0:32, :] = back[w]
+        out[w, 32:40, :] = tile
+
+
+def update_kernel(recv, lag, obs, inc, zobs, lag_out, obs_out, inc_out):
+    total = recv[0, 32:33, :]
+    for w in range(1, NW):
+        total = total + recv[w, 32:33, :]
     lane = lax.broadcasted_iota(jnp.int32, (1, HALF), 1)
     cross = jnp.sum(jnp.where(lane < HALF // 2, total, 0.0), axis=1, keepdims=True)
     square = jnp.sum(jnp.where(lane < HALF // 2, 0.0, total), axis=1, keepdims=True)
@@ -247,24 +249,29 @@
         name="outer_runs",
     )(first_tiles, last_tiles, nxt, prv, *inner)
     recv = lax.all_to_all(send, "tm", 0, 0)
-    back = call(sum_kernel, sds((NW, 40, HALF), F32), [VMEM] * 2, VMEM, name="window_sums")(recv, part)
+    back, sums = call(
+        functools.partial(sum_kernel, size),
+        (sds((NW, 32, HALF), F32), sds((size, 1, HALF), F32)),
+        [VMEM] * 2,
+        (VMEM, VMEM),
+        name="window_sums",
+    )(recv, part)
+    sums = lax.all_to_all(sums, "space", 0, 0)
+    back = call(
+        functools.partial(join_kernel, size),
+        sds((NW, 40, HALF), F32),
+        [VMEM] * 2,
+        VMEM,
+        name="join",
+    )(sums, back)
     back = lax.all_to_all(back, "tm", 0, 0)
-    sums = call(
-        functools.partial(scalar_kernel, size),
-        sds((size, 1, HALF), F32),
-        [pl.BlockSpec((NW, 8, HALF), lambda i: (0, 4, 0))],
-        pl.BlockSpec((size, 1, HALF), lambda i: (0, 0, 0)),
-        grid=(1,),
-        name="scalars",
-    )(back)
-    sums = lax.all_to_all(sums, "space", 0, 0)
     return call(
-        functools.partial(update_kernel, size),
+        update_kernel,
         (sds(lag.shape, F32), sds(obs.shape, F32), sds(inc.shape, F32)),
-        [VMEM] * 6,
+        [VMEM] * 5,
         (VMEM, VMEM, VMEM),
         name="update",
-    )(sums, back, lag, obs, inc, zobs)
+    )(back, lag, obs, inc, zobs)
 
 
 def solution(mesh):

time: 68.1 us -> 66.5 us (0.977)
  blocking collectives: 52.5 us -> 50.9 us
    all_to_all x1, blocking collectives: 26.3 us -> 24.5 us  [body(): sums = lax.all_to_all(sums, 'space', 0, 0)]
where the time goes in v4:
time: 66.5 us; the launch traced here: 66.1 us
  blocking collectives  50.9 us (77%)
  starting transfers between devices  6.89 us (10%)
  Pallas kernels  6.01 us (9%)
  waiting for transfers between devices  1.6 us (2%)
  between operations  0.69 us (1%)
    all_to_all x1, blocking collectives, body(): sums = lax.all_to_all(sums, 'space', 0, 0)  24.5 us
    all_to_all x1, blocking collectives, body(): recv = lax.all_to_all(send, 'tm', 0, 0)  15.5 us
    all_to_all x1, blocking collectives, body(): back = lax.all_to_all(back, 'tm', 0, 0)  10.9 us
    ppermute x1, starting transfers between devices, body(): lax.ppermute(first, 'space', [((i + 1) % size, i) for i in range(size)])  6.89 us
    pallas_call x1, Pallas kernels, body(): call(inner_kernel, (one, four, two, two), [VMEM] * 10, (VMEM,) * 4, name=...  2.76 us
    ppermute x1, waiting for transfers between devices, body(): lax.ppermute(last, 'space', [(i, (i + 1) % size) for i in range(size)])  1.6 us
  transfers between devices with their start and end apart: 2, of which 1 were waited for; matrix products, arithmetic and copies ran while one was open for 0% of the time, Pallas kernels for 4%

profile of v4, /device:TPU:1, one launch (start us, length us, event | category | flops | bytes accessed | tf_op | source)
XLA Modules:
  0.0 66.1 jit_solution(1379119308697802359)
XLA Ops:
  0.6 1.1 %edges.1 = (f32[112,256]{1,0:T(8,128)S(1)}, f32[112,256]{1,0:T(8,128)S(1)}, f32[7,4,8,256]{3,2,1,0:T(8,128)S(1)}, f32[7,4,8,256]{3,2,1,0:T(8,128)S(1)}) custom-call(f32[1,4,32,256]{3,2,1,0:T(8,128)} %lag.5, f32[1,2,4,32,256]{4,3,2,1,0:T(8,128)} %obs.5, f32[1,4,32,256]{3,2,1,0:T(8,128)} %inc.5, f32[4,32,256]{2,1,0:T(8,128)} %cx.3, f32[4,32,256]{2,1,0:T(8,128)} %cy.3, ...), custom_call_target="tpu_custom_call" | custom-call | tf_op jit(solution)/shard_map/edges/pallas_call | solution.py:226
  1.8 6.9 %collective-permute-start = (f32[112,256]{1,0:T(8,128)S(1)}, f32[112,256]{1,0:T(8,128)S(1)}, u32[]{:S(2)}, u32[]{:S(2)}) collective-permute-start(f32[112,256]{1,0:T(8,128)S(1)} %get-tuple-element.18), channel_id=1, source_target_pairs={{1,0},{2,1},{3,2},{4,3},{5,4},{6,5},{7,6},{8,7},{9,8},{10,9},{11,1... | collective-permute-start | bytes 344072 | tf_op jit(solution)/shard_map/ppermute | solution.py:234
  8.7 0.0 collective-permute-start.1
  8.7 2.8 %inner_runs.1 = (f32[4,32,256]{2,1,0:T(8,128)S(1)}, f32[4,4,32,256]{3,2,1,0:T(8,128)S(1)}, f32[2,4,32,256]{3,2,1,0:T(8,128)S(1)}, f32[2,4,32,256]{3,2,1,0:T(8,128)S(1)}) custom-call(f32[1,4,32,256]{3,2,1,0:T(8,128)} %lag.5, f32[1,2,4,32,256]{4,3,2,1,0:T(8,128)} %obs.5, f32[1,4,32,256]{3,2,1,0:T(8,128)} %inc.5, f32[1,4,32,256]{3,2,1,0:T(8,128)} %mside.1, ...), custom_call_target="tpu_custom_call" | custom-call | flops 8388608 | bytes 4194304 | tf_op jit(solution)/shard_map/inner_runs/pallas_call | solution.py:236
  11.4 0.0 collective-permute-done.nxt
  11.4 1.6 %collective-permute-done.1.prv = f32[112,256]{1,0:T(8,128)S(1)} collective-permute-done((f32[112,256]{1,0:T(8,128)S(1)}, f32[112,256]{1,0:T(8,128)S(1)}, u32[]{:S(2)}, u32[]{:S(2)}) %collective-permute-start.1) | collective-permute-done | bytes 114720 | tf_op jit(solution)/shard_map/ppermute | solution.py:235
  13.0 1.0 %outer_runs.1 = (f32[16,32,256]{2,1,0:T(8,128)S(1)}, f32[2,4,32,256]{3,2,1,0:T(8,128)S(1)}, f32[2,8,256]{2,1,0:T(8,128)S(1)}) custom-call(f32[7,4,8,256]{3,2,1,0:T(8,128)S(1)} %get-tuple-element.16.first, f32[7,4,8,256]{3,2,1,0:T(8,128)S(1)} %get-tuple-element.17.last, f32[112,256]{1,0:T(8,128)S(1)} %collective-permute-done.nxt, ...), custom_call_target="tpu_custom_call" | custom-call | tf_op jit(solution)/shard_map/outer_runs/pallas_call | solution.py:244
  14.1 15.5 %all_to_all.15.recv = f32[16,32,256]{2,1,0:T(8,128)S(1)} all-to-all(f32[16,32,256]{2,1,0:T(8,128)S(1)} %get-tuple-element.24), channel_id=1, replica_groups=mesh['tm'=16,'space'=32] {'tm'}, dimensions={0} | all-to-all | bytes 1048576 | tf_op jit(solution)/shard_map/all_to_all | solution.py:251
  29.6 0.2 window_sums.1
  29.8 24.5 %all_to_all.16.sums = f32[32,1,128]{2,1,0:T(1,128)S(1)} all-to-all(f32[32,1,128]{2,1,0:T(1,128)S(1)} %get-tuple-element.26), channel_id=1, replica_groups=mesh['tm'=16,'space'=32] {'space'}, dimensions={0} | all-to-all | bytes 32768 | tf_op jit(solution)/shard_map/all_to_all | solution.py:259
  54.3 0.0 copy-start
  54.3 0.0 copy-start.1
  54.3 0.0 copy-start.2
  54.3 10.9 %all_to_all.17.recv = f32[16,40,128]{2,1,0:T(8,128)S(1)} all-to-all(f32[16,40,128]{2,1,0:T(8,128)S(1)} %join.1), channel_id=1, replica_groups=mesh['tm'=16,'space'=32] {'tm'}, dimensions={0} | all-to-all | bytes 655360 | tf_op jit(solution)/shard_map/all_to_all | solution.py:267
  65.2 0.0 copy-done
  65.2 0.0 copy-done.1
  65.2 0.0 copy-done.2
  65.2 0.9 %update.1 = (f32[1,4,32,256]{3,2,1,0:T(8,128)}, f32[1,2,4,32,256]{4,3,2,1,0:T(8,128)}, f32[1,4,32,256]{3,2,1,0:T(8,128)}) custom-call(f32[16,40,128]{2,1,0:T(8,128)S(1)} %all_to_all.17.recv, f32[1,4,32,256]{3,2,1,0:T(8,128)S(1)} %copy-done.1, f32[1,2,4,32,256]{4,3,2,1,0:T(8,128)S(1)} %copy-done, f32[1,4,32,256]{3,2,1,0:T(8,128)S(1)} %copy-done.2, ...), custom_call_target="tpu_custom_call" | custom-call | tf_op jit(solution)/shard_map/update/pallas_call | solution.py:268
  (1 shorter events, 0.0 us)
Async XLA Ops:
  1.8 9.7 %collective-permute-start = (f32[112,256]{1,0:T(8,128)S(1)}, f32[112,256]{1,0:T(8,128)S(1)}, u32[]{:S(2)}, u32[]{:S(2)}) collective-permute-start(f32[112,256]{1,0:T(8,128)S(1)} %get-tuple-element.18), channel_id=1, source_target_pairs={{1,0},{2,1},{3,2},{4,3},{5,4},{6,5},{7,6},{8,7},{9,8},{10,9},{11,1... | collective-permute-start | bytes 344072 | tf_op jit(solution)/shard_map/ppermute | solution.py:234
  8.7 4.4 %collective-permute-start.1 = (f32[112,256]{1,0:T(8,128)S(1)}, f32[112,256]{1,0:T(8,128)S(1)}, u32[]{:S(2)}, u32[]{:S(2)}) collective-permute-start(f32[112,256]{1,0:T(8,128)S(1)} %get-tuple-element.19), channel_id=1, source_target_pairs={{0,1},{1,2},{2,3},{3,4},{4,5},{5,6},{6,7},{7,8},{8,9},{9,10},{10,1... | collective-permute-start | bytes 344072 | tf_op jit(solution)/shard_map/ppermute | solution.py:235
  54.3 10.9 %copy-start = (f32[1,2,4,32,256]{4,3,2,1,0:T(8,128)S(1)}, f32[1,2,4,32,256]{4,3,2,1,0:T(8,128)}, u32[]{:S(2)}) copy-start(f32[1,2,4,32,256]{4,3,2,1,0:T(8,128)} %obs.5) | copy-start | bytes 786436
  54.3 10.9 %copy-start.1 = (f32[1,4,32,256]{3,2,1,0:T(8,128)S(1)}, f32[1,4,32,256]{3,2,1,0:T(8,128)}, u32[]{:S(2)}) copy-start(f32[1,4,32,256]{3,2,1,0:T(8,128)} %lag.5) | copy-start | bytes 393220
  54.3 10.9 %copy-start.2 = (f32[1,4,32,256]{3,2,1,0:T(8,128)S(1)}, f32[1,4,32,256]{3,2,1,0:T(8,128)}, u32[]{:S(2)}) copy-start(f32[1,4,32,256]{3,2,1,0:T(8,128)} %inc.5) | copy-start | bytes 393220

commit v5 on v4

--- a/solution.py
+++ b/solution.py
@@ -32,10 +32,6 @@
     )
 
 
-def lower_half(shape):
-    return lax.broadcasted_iota(jnp.int32, shape, 0) < 4
-
-
 def edge_kernel(lag, obs, inc, cx, cy, df, first_out, last_out, first, last, sem):
     sources = [inc.at[0], obs.at[0, 1], obs.at[0, 0], lag.at[0], cx, cy, df]
     copies = []
@@ -46,7 +42,7 @@
         c.start()
     for c in copies:
         c.wait()
-    low = lower_half((8, NY))
+    low = lax.broadcasted_iota(jnp.int32, (8, NY), 0) < 4
     for f in range(EDGE):
         for m in range(2):
             k = 8 * (2 * f + m)
@@ -54,21 +50,8 @@
             last_out[k : k + 8, :] = jnp.where(low, pltpu.roll(last[f, 2 * m], 4, 0), last[f, 2 * m + 1])
 
 
-def halo(nxt, prv, f, l):
-    k = 8 * (2 * f + l // 2)
-    low = lower_half((8, NY))
-    a, b = nxt[k : k + 8, :], prv[k : k + 8, :]
-    if l % 2 == 0:
-        return jnp.where(low, a, pltpu.roll(b, 4, 0))
-    return jnp.where(low, pltpu.roll(a, 4, 0), b)
-
-
-def east(x):
-    return pltpu.roll(x, x.shape[0] - 1, 0)
-
-
-def west(x):
-    return pltpu.roll(x, 1, 0)
+def turn(x, rows):
+    return pltpu.roll(x, rows % x.shape[0], 0)
 
 
 def north(x):
@@ -79,43 +62,48 @@
     return pltpu.roll(x, 1, 1)
 
 
-def tangent(q, c):
-    a0, ae, aw, an, as_ = c
-    return a0 * q + ae * east(q) + aw * west(q) + an * north(q) + as_ * south(q)
-
-
-def adjoint(p, c):
-    a0, ae, aw, an, as_ = c
-    return a0 * p + east(aw * p) + west(ae * p) + north(as_ * p) + south(an * p)
-
-
-def runs(inc, obs1, obs0, lag, x, y, d):
-    col = lax.broadcasted_iota(jnp.int32, d.shape, 1)
-    x, y = 0.5 * x, 0.5 * y
-    coefs = (
-        1.0 - 4.0 * d,
-        d - x,
-        d + x,
-        jnp.where(col == NY - 1, 0.0, d - y),
-        jnp.where(col == 0, 0.0, d + y),
-    )
-    q, p, b = inc, obs1, lag
-    for step in range(STEPS):
-        if step == STEPS // 2:
-            middle = q
-            p = p + obs0
-        q = tangent(q, coefs)
-        p = adjoint(p, coefs)
-        b = adjoint(b, coefs)
-    return middle, q, p, b
-
-
-def inner_kernel(lag, obs, inc, mside, oside, mvar, ovar, cx, cy, df, fixed, states, resid, inverse):
+def weights(cx, cy, df):
+    col = lax.broadcasted_iota(jnp.int32, df.shape, 1)
+    x, y = 0.5 * cx, 0.5 * cy
+    an = jnp.where(col == NY - 1, 0.0, df - y)
+    as_ = jnp.where(col == 0, 0.0, df + y)
+    return 1.0 - 4.0 * df, df - x, df + x, an, as_
+
+
+def along_y(p, c):
+    return c[0] * p + north(c[4] * p) + south(c[3] * p)
+
+
+def inner_kernel(lag, obs, inc, mside, oside, mvar, ovar, cx, cy, df, fixed, states, resid, inverse, feed):
+    tile_row = lax.broadcasted_iota(jnp.int32, (8, NY), 0)
+    row = lax.broadcasted_iota(jnp.int32, (ROWS, NY), 0)
+
+    def hand_over(l, run, step, up, down):
+        m, h = l // 2, 4 * (l % 2)
+        for side, (x, at, to) in enumerate(((up, 7, h + step + 1), (down, 0, h + 2 - step))):
+            other = 0.0 if h == 0 else feed[side, run, step, m]
+            feed[side, run, step, m] = jnp.where(tile_row == to, turn(x, to - at), other)
+
     for l in range(LEV):
+        a0, ae_full, aw_full, an, as_ = c = weights(cx[l], cy[l], df[l])
+        ae = jnp.where(row == ROWS - 1, 0.0, ae_full)
+        aw = jnp.where(row == 0, 0.0, aw_full)
         lagr = lag[0, l]
-        out = runs(inc[0, l], obs[0, 1, l], obs[0, 0, l], lagr, cx[l], cy[l], df[l])
-        for i in range(4):
-            states[i, l] = out[i] + lagr if i == 2 else out[i]
+        q, p, b = inc[0, l], obs[0, 1, l], lagr
+        for step in range(STEPS):
+            if step == STEPS // 2:
+                states[0, l] = q
+                p = p + obs[0, 0, l]
+            if step < STEPS - 1:
+                hand_over(l, 0, step, q[ROWS - 8 :], q[:8])
+                for run, x in ((1, p), (2, b)):
+                    hand_over(l, run, step, ae_full[ROWS - 8 :] * x[ROWS - 8 :], aw_full[:8] * x[:8])
+            q = a0 * q + ae * turn(q, -1) + aw * turn(q, 1) + an * north(q) + as_ * south(q)
+            p = along_y(p, c) + turn(aw * p, -1) + turn(ae * p, 1)
+            b = along_y(b, c) + turn(aw * b, -1) + turn(ae * b, 1)
+        states[1, l] = q
+        states[2, l] = p + lagr
+        states[3, l] = b
         fixed[l] = mside[0, l] - mvar[0, l] * lagr - inc[0, l]
         for j in range(2):
             var = ovar[0, j, l]
@@ -123,31 +111,84 @@
             inverse[j, l] = 1.0 / var
 
 
-def outer_kernel(first, last, nxt, prv, fixed, states, resid, inverse, send, zobs, part):
-    low = lower_half((8, NY))
+def added(side, m, first, last, nxt, prv, feed):
+    i = lax.broadcasted_iota(jnp.int32, (8, NY), 0) & 3
+    inward = 1 - 2 * side
+
+    def tile(ref, f):
+        k = 8 * (2 * f + m)
+        return ref[k : k + 8, :]
+
+    def rows(f, s):
+        outer, inner = (nxt, last) if side == 0 else (prv, first)
+        if s == 0:
+            return tile(outer, f)
+        if s == 4:
+            return tile(inner, f)
+        own = i < s if side == 0 else i >= 4 - s
+        return jnp.where(own, turn(tile(inner, f), inward * (s - 4)), turn(tile(outer, f), inward * s))
+
+    def moved(x, n):
+        keep = i >= n if side == 0 else i < 4 - n
+        return jnp.where(keep, turn(x, inward * n), 0.0)
+
+    q, p, b = tile(nxt if side == 0 else prv, 0), rows(1, 0), rows(3, 0)
+    here = weights(rows(4, 0), rows(5, 0), rows(6, 0))
+    for s in range(STEPS):
+        if s == STEPS // 2:
+            middle = q
+            p = p + moved(rows(2, 0), 2)
+        there = weights(rows(4, s + 1), rows(5, s + 1), rows(6, s + 1))
+        a0, ae, aw, an, as_ = there
+        ahead, behind = (ae, aw) if side == 0 else (aw, ae)
+        mid = moved(q, 1)
+        past = moved(q, 2)
+        if s < STEPS - 1:
+            past = past + feed[side, 0, s, m]
+        q = a0 * mid + ahead * q + behind * past + an * north(mid) + as_ * south(mid)
+        ahead, behind = (here[2], here[1]) if side == 0 else (here[1], here[2])
+        out = []
+        for run, x in ((1, p), (2, b)):
+            y = moved(along_y(x, here), 1) + ahead * x + moved(behind * x, 2)
+            if s < STEPS - 1:
+                y = y + feed[side, run, s, m]
+            out.append(y)
+        p, b = out
+        here = there
+    return middle, q, p, b
+
+
+def outer_kernel(first, last, nxt, prv, fixed, states, resid, inverse, feed, send, zobs, part):
+    row = lax.broadcasted_iota(jnp.int32, (8, NY), 0)
     cross = jnp.zeros((8, NY), F32)
     square = jnp.zeros((8, NY), F32)
-    for l in range(LEV):
-        ring = [jnp.concatenate([last[f, l], halo(nxt, prv, f, l), first[f, l]], axis=0) for f in range(EDGE)]
-        out = list(runs(*ring))
-        out[2] = out[2] + ring[3]
-        for k in range(4):
-            rows = slice(8 * k, 8 * k + 8)
-            tiles = [states[i, l, rows, :] for i in range(4)]
-            if k == 0:
-                tiles = [jnp.where(low, o[16:24], v) for o, v in zip(out, tiles)]
-            if k == 3:
-                tiles = [jnp.where(low, v, o[0:8]) for o, v in zip(out, tiles)]
-            t = 4 * l + k
-            send[t, 0:8, :] = fixed[l, rows, :]
-            for i in range(1, 4):
-                send[t, 8 * i : 8 * i + 8, :] = tiles[i]
-            for j in range(2):
-                r = resid[j, l, rows, :] - tiles[j]
-                z = r * inverse[j, l, rows, :]
-                zobs[j, l, rows, :] = z
-                cross = cross + r * z
-                square = square + z * z
+    for m in range(2):
+        more = [added(side, m, first, last, nxt, prv, feed) for side in range(2)]
+        for h in range(2):
+            l = 2 * m + h
+            for k in range(4):
+                rows = slice(8 * k, 8 * k + 8)
+                tiles = [states[n, l, rows, :] for n in range(4)]
+                if k == 0:
+                    mid, *end = more[1]
+                    tiles[0] = tiles[0] + jnp.where(row < 2, turn(mid, -2 - 4 * h), 0.0)
+                    for n in range(3):
+                        tiles[n + 1] = tiles[n + 1] + jnp.where(row < 4, turn(end[n], -4 * h), 0.0)
+                if k == 3:
+                    mid, *end = more[0]
+                    tiles[0] = tiles[0] + jnp.where(row >= 6, turn(mid, 6 - 4 * h), 0.0)
+                    for n in range(3):
+                        tiles[n + 1] = tiles[n + 1] + jnp.where(row >= 4, turn(end[n], 4 - 4 * h), 0.0)
+                t = 4 * l + k
+                send[t, 0:8, :] = fixed[l, rows, :]
+                for n in range(1, 4):
+                    send[t, 8 * n : 8 * n + 8, :] = tiles[n]
+                for j in range(2):
+                    r = resid[j, l, rows, :] - tiles[j]
+                    z = r * inverse[j, l, rows, :]
+                    zobs[j, l, rows, :] = z
+                    cross = cross + r * z
+                    square = square + z * z
     part[0] = cross
     part[1] = square
 
@@ -220,34 +261,34 @@
     sds = jax.ShapeDtypeStruct
     size = lax.axis_size("space")
     edge = sds((EDGE * LEV * 4, NY), F32)
-    tiles = sds((EDGE, LEV, 8, NY), F32)
     one, two, four = (sds(n + (LEV, ROWS, NY), F32) for n in ((), (2,), (4,)))
+    feed = sds((2, 3, STEPS - 1, LEV // 2, 8, NY), F32)
     held = [pltpu.with_memory_space_constraint(x, pltpu.HBM) for x in (lag, obs, inc, mside, oside, mvar, ovar, cx, cy, df)]
-    first, last, first_tiles, last_tiles = call(
+    first, last = call(
         edge_kernel,
-        (edge, edge, tiles, tiles),
+        (edge, edge),
         [ANY] * 6,
-        (VMEM,) * 4,
-        [pltpu.SemaphoreType.DMA((2 * EDGE,))],
+        (VMEM,) * 2,
+        [pltpu.VMEM((EDGE, LEV, 8, NY), F32)] * 2 + [pltpu.SemaphoreType.DMA((2 * EDGE,))],
         name="edges",
     )(*held[:3], *held[7:])
     nxt = lax.ppermute(first, "space", [((i + 1) % size, i) for i in range(size)])
     prv = lax.ppermute(last, "space", [(i, (i + 1) % size) for i in range(size)])
     inner = call(
         inner_kernel,
-        (one, four, two, two),
+        (one, four, two, two, feed),
         [VMEM] * 10,
-        (VMEM,) * 4,
+        (VMEM,) * 5,
         name="inner_runs",
         cost_estimate=pl.CostEstimate(flops=8 * 1024 * 1024, bytes_accessed=4 * 1024 * 1024, transcendentals=0),
     )(*held)
     send, zobs, part = call(
         outer_kernel,
         (sds((NW, 32, NY), F32), two, sds((2, 8, NY), F32)),
-        [VMEM] * 8,
+        [VMEM] * 9,
         (VMEM, VMEM, VMEM),
         name="outer_runs",
-    )(first_tiles, last_tiles, nxt, prv, *inner)
+    )(first, last, nxt, prv, *inner)
     recv = lax.all_to_all(send, "tm", 0, 0)
     back, sums = call(
         functools.partial(sum_kernel, size),

time: 66.5 us -> 65.9 us (level)
  no operation moved by 1% of the time
where the time goes in v5:
time: 65.9 us; the launch traced here: 65.6 us
  blocking collectives  51 us (77%)
  starting transfers between devices  6.89 us (10%)
  Pallas kernels  5.46 us (8%)
  waiting for transfers between devices  1.57 us (2%)
  between operations  0.69 us (1%)
    all_to_all x1, blocking collectives, body(): sums = lax.all_to_all(sums, 'space', 0, 0)  24.5 us
    all_to_all x1, blocking collectives, body(): recv = lax.all_to_all(send, 'tm', 0, 0)  15.5 us
    all_to_all x1, blocking collectives, body(): back = lax.all_to_all(back, 'tm', 0, 0)  10.9 us
    ppermute x1, starting transfers between devices, body(): lax.ppermute(first, 'space', [((i + 1) % size, i) for i in range(size)])  6.89 us
    pallas_call x1, Pallas kernels, body(): call(inner_kernel, (one, four, two, two, feed), [VMEM] * 10, (VMEM,) * 5,...  2.79 us
    ppermute x1, waiting for transfers between devices, body(): lax.ppermute(last, 'space', [(i, (i + 1) % size) for i in range(size)])  1.56 us
  transfers between devices with their start and end apart: 2, of which 1 were waited for; matrix products, arithmetic and copies ran while one was open for 0% of the time, Pallas kernels for 4%

profile of v5, /device:TPU:1, one launch (start us, length us, event | category | flops | bytes accessed | tf_op | source)
XLA Modules:
  0.0 65.6 jit_solution(14999545868060059777)
XLA Ops:
  0.6 1.1 %edges.1 = (f32[112,256]{1,0:T(8,128)S(1)}, f32[112,256]{1,0:T(8,128)S(1)}) custom-call(f32[1,4,32,256]{3,2,1,0:T(8,128)} %lag.5, f32[1,2,4,32,256]{4,3,2,1,0:T(8,128)} %obs.5, f32[1,4,32,256]{3,2,1,0:T(8,128)} %inc.5, f32[4,32,256]{2,1,0:T(8,128)} %cx.3, f32[4,32,256]{2,1,0:T(8,128)} %cy.3, f32[4,32,256]{2,1,0:T(8,128)} %df.3), custom_call_target="tpu_custom_call" | custom-call | tf_op jit(solution)/shard_map/edges/pallas_call | solution.py:267
  1.8 6.9 %collective-permute-start = (f32[112,256]{1,0:T(8,128)S(1)}, f32[112,256]{1,0:T(8,128)S(1)}, u32[]{:S(2)}, u32[]{:S(2)}) collective-permute-start(f32[112,256]{1,0:T(8,128)S(1)} %get-tuple-element.15.first), channel_id=1, source_target_pairs={{1,0},{2,1},{3,2},{4,3},{5,4},{6,5},{7,6},{8,7},{9,8},{10,9},{11,1... | collective-permute-start | bytes 344072 | tf_op jit(solution)/shard_map/ppermute | solution.py:275
  8.6 0.0 collective-permute-start.1
  8.7 2.8 %inner_runs.1 = (f32[4,32,256]{2,1,0:T(8,128)S(1)}, f32[4,4,32,256]{3,2,1,0:T(8,128)S(1)}, f32[2,4,32,256]{3,2,1,0:T(8,128)S(1)}, f32[2,4,32,256]{3,2,1,0:T(8,128)S(1)}, f32[2,3,3,2,8,256]{5,4,3,2,1,0:T(8,128)S(1)}) custom-call(f32[1,4,32,256]{3,2,1,0:T(8,128)} %lag.5, f32[1,2,4,32,256]{4,3,2,1,0:T(8,128)} %obs.5, f32[1,4,32,256]{3,2,1,0:T(8,128)} %inc.5, ...), custom_call_target="tpu_custom_call" | custom-call | flops 8388608 | bytes 4194304 | tf_op jit(solution)/shard_map/inner_runs/pallas_call | solution.py:277
  11.5 0.0 collective-permute-done.nxt
  11.5 1.6 %collective-permute-done.1.prv = f32[112,256]{1,0:T(8,128)S(1)} collective-permute-done((f32[112,256]{1,0:T(8,128)S(1)}, f32[112,256]{1,0:T(8,128)S(1)}, u32[]{:S(2)}, u32[]{:S(2)}) %collective-permute-start.1) | collective-permute-done | bytes 114720 | tf_op jit(solution)/shard_map/ppermute | solution.py:276
  13.0 0.4 outer_runs.1
  13.5 15.5 %all_to_all.15.recv = f32[16,32,256]{2,1,0:T(8,128)S(1)} all-to-all(f32[16,32,256]{2,1,0:T(8,128)S(1)} %get-tuple-element.22), channel_id=1, replica_groups=mesh['tm'=16,'space'=32] {'tm'}, dimensions={0} | all-to-all | bytes 1048576 | tf_op jit(solution)/shard_map/all_to_all | solution.py:292
  29.0 0.2 window_sums.1
  29.2 24.5 %all_to_all.16.sums = f32[32,1,128]{2,1,0:T(1,128)S(1)} all-to-all(f32[32,1,128]{2,1,0:T(1,128)S(1)} %get-tuple-element.24), channel_id=1, replica_groups=mesh['tm'=16,'space'=32] {'space'}, dimensions={0} | all-to-all | bytes 32768 | tf_op jit(solution)/shard_map/all_to_all | solution.py:300
  53.7 0.0 copy-start
  53.7 0.0 copy-start.1
  53.8 0.0 copy-start.2
  53.8 10.9 %all_to_all.17.recv = f32[16,40,128]{2,1,0:T(8,128)S(1)} all-to-all(f32[16,40,128]{2,1,0:T(8,128)S(1)} %join.1), channel_id=1, replica_groups=mesh['tm'=16,'space'=32] {'tm'}, dimensions={0} | all-to-all | bytes 655360 | tf_op jit(solution)/shard_map/all_to_all | solution.py:308
  64.7 0.0 copy-done
  64.7 0.0 copy-done.1
  64.7 0.0 copy-done.2
  64.7 0.9 %update.1 = (f32[1,4,32,256]{3,2,1,0:T(8,128)}, f32[1,2,4,32,256]{4,3,2,1,0:T(8,128)}, f32[1,4,32,256]{3,2,1,0:T(8,128)}) custom-call(f32[16,40,128]{2,1,0:T(8,128)S(1)} %all_to_all.17.recv, f32[1,4,32,256]{3,2,1,0:T(8,128)S(1)} %copy-done.1, f32[1,2,4,32,256]{4,3,2,1,0:T(8,128)S(1)} %copy-done, f32[1,4,32,256]{3,2,1,0:T(8,128)S(1)} %copy-done.2, ...), custom_call_target="tpu_custom_call" | custom-call | tf_op jit(solution)/shard_map/update/pallas_call | solution.py:309
  (1 shorter events, 0.0 us)
Async XLA Ops:
  1.8 9.7 %collective-permute-start = (f32[112,256]{1,0:T(8,128)S(1)}, f32[112,256]{1,0:T(8,128)S(1)}, u32[]{:S(2)}, u32[]{:S(2)}) collective-permute-start(f32[112,256]{1,0:T(8,128)S(1)} %get-tuple-element.15.first), channel_id=1, source_target_pairs={{1,0},{2,1},{3,2},{4,3},{5,4},{6,5},{7,6},{8,7},{9,8},{10,9},{11,1... | collective-permute-start | bytes 344072 | tf_op jit(solution)/shard_map/ppermute | solution.py:275
  8.6 4.4 %collective-permute-start.1 = (f32[112,256]{1,0:T(8,128)S(1)}, f32[112,256]{1,0:T(8,128)S(1)}, u32[]{:S(2)}, u32[]{:S(2)}) collective-permute-start(f32[112,256]{1,0:T(8,128)S(1)} %get-tuple-element.16.last), channel_id=1, source_target_pairs={{0,1},{1,2},{2,3},{3,4},{4,5},{5,6},{6,7},{7,8},{8,9},{9,10},{10,1... | collective-permute-start | bytes 344072 | tf_op jit(solution)/shard_map/ppermute | solution.py:276
  53.7 11.0 %copy-start = (f32[1,2,4,32,256]{4,3,2,1,0:T(8,128)S(1)}, f32[1,2,4,32,256]{4,3,2,1,0:T(8,128)}, u32[]{:S(2)}) copy-start(f32[1,2,4,32,256]{4,3,2,1,0:T(8,128)} %obs.5) | copy-start | bytes 786436
  53.7 10.9 %copy-start.1 = (f32[1,4,32,256]{3,2,1,0:T(8,128)S(1)}, f32[1,4,32,256]{3,2,1,0:T(8,128)}, u32[]{:S(2)}) copy-start(f32[1,4,32,256]{3,2,1,0:T(8,128)} %lag.5) | copy-start | bytes 393220
  53.8 10.9 %copy-start.2 = (f32[1,4,32,256]{3,2,1,0:T(8,128)S(1)}, f32[1,4,32,256]{3,2,1,0:T(8,128)}, u32[]{:S(2)}) copy-start(f32[1,4,32,256]{3,2,1,0:T(8,128)} %inc.5) | copy-start | bytes 393220

commit v6 on v5

--- a/solution.py
+++ b/solution.py
@@ -15,6 +15,12 @@
 HALF = 128
 EDGE = 7
 F32 = jnp.float32
+
+SPACE_ORDER = [2 * (z % 16) + core for z in range(26, 10, -1) for core in (1, 0)]
+OUT_ORDER = [10, 6, 9, 11, 14, 2, 5, 7, 8, 13, 15, 1, 3, 4, 12, 0]
+BACK_ORDER = OUT_ORDER
+OUT_AT = [OUT_ORDER.index(w) for w in range(NW)]
+BACK_AT = [BACK_ORDER.index(w) for w in range(NW)]
 
 VMEM = pl.BlockSpec(memory_space=pltpu.VMEM)
 ANY = pl.BlockSpec(memory_space=pl.ANY)
@@ -179,7 +185,7 @@
                     tiles[0] = tiles[0] + jnp.where(row >= 6, turn(mid, 6 - 4 * h), 0.0)
                     for n in range(3):
                         tiles[n + 1] = tiles[n + 1] + jnp.where(row >= 4, turn(end[n], 4 - 4 * h), 0.0)
-                t = 4 * l + k
+                t = OUT_AT[4 * l + k]
                 send[t, 0:8, :] = fixed[l, rows, :]
                 for n in range(1, 4):
                     send[t, 8 * n : 8 * n + 8, :] = tiles[n]
@@ -198,23 +204,25 @@
     z = jnp.zeros((8, NY), F32)
     before = jnp.zeros((8, NY), F32)
     for w in range(NW):
-        r = recv[w, 0:8, :] + before
-        before = recv[w, 8:16, :]
+        i, o = OUT_AT[w], BACK_AT[w]
+        r = recv[i, 0:8, :] + before
+        before = recv[i, 8:16, :]
         z = z + r
         cross = cross + r * z
         square = square + z * z
-        back[w, 0:8, :] = z[:, :HALF]
-        back[w, 8:16, :] = z[:, HALF:]
+        back[o, 0:8, :] = z[:, :HALF]
+        back[o, 8:16, :] = z[:, HALF:]
     z = jnp.zeros((8, NY), F32)
     after = jnp.zeros((8, NY), F32)
     for w in reversed(range(NW)):
-        r = after - recv[w, 16:24, :]
-        after = recv[w, 24:32, :]
+        i, o = OUT_AT[w], BACK_AT[w]
+        r = after - recv[i, 16:24, :]
+        after = recv[i, 24:32, :]
         z = z + r
         cross = cross + r * z
         square = square + z * z
-        back[w, 16:24, :] = z[:, :HALF]
-        back[w, 24:32, :] = z[:, HALF:]
+        back[o, 16:24, :] = z[:, :HALF]
+        back[o, 24:32, :] = z[:, HALF:]
 
     def fold(v):
         v = v[:, :HALF] + v[:, HALF:]
@@ -248,7 +256,7 @@
     for l in range(LEV):
         for k in range(4):
             rows = slice(8 * k, 8 * k + 8)
-            t = 4 * l + k
+            t = BACK_AT[4 * l + k]
             for h in range(2):
                 cols = slice(HALF * h, HALF * h + HALF)
                 lag_out[0, l, rows, cols] = lag[0, l, rows, cols] + step * recv[t, 8 * h : 8 * h + 8, :]
@@ -289,7 +297,7 @@
         (VMEM, VMEM, VMEM),
         name="outer_runs",
     )(first, last, nxt, prv, *inner)
-    recv = lax.all_to_all(send, "tm", 0, 0)
+    recv = lax.all_to_all(send, "tm", 0, 0, axis_index_groups=[OUT_ORDER])
     back, sums = call(
         functools.partial(sum_kernel, size),
         (sds((NW, 32, HALF), F32), sds((size, 1, HALF), F32)),
@@ -297,7 +305,7 @@
         (VMEM, VMEM),
         name="window_sums",
     )(recv, part)
-    sums = lax.all_to_all(sums, "space", 0, 0)
+    sums = lax.all_to_all(sums, "space", 0, 0, axis_index_groups=[SPACE_ORDER])
     back = call(
         functools.partial(join_kernel, size),
         sds((NW, 40, HALF), F32),
@@ -305,7 +313,7 @@
         VMEM,
         name="join",
     )(sums, back)
-    back = lax.all_to_all(back, "tm", 0, 0)
+    back = lax.all_to_all(back, "tm", 0, 0, axis_index_groups=[BACK_ORDER])
     return call(
         update_kernel,
         (sds(lag.shape, F32), sds(obs.shape, F32), sds(inc.shape, F32)),

time: 65.9 us -> 58.5 us (0.89)
  blocking collectives: 51 us -> 43.5 us
    all_to_all x3, blocking collectives: 51 us -> 43.5 us  [the longest x1 19.8 us: body(): sums = lax.all_to_all(sums, 'space', 0, 0, axis_index_groups=[SPACE_ORDER])]
  transfers between devices with their start and end apart: 2 -> 2, of which waited for: 1 -> 1; matrix products, arithmetic and copies ran while one was open for 0% -> 0% of each run, Pallas kernels for 4% -> 5%
where the time goes in v6:
time: 58.5 us; the launch traced here: 58.1 us
  blocking collectives  43.5 us (74%)
  starting transfers between devices  6.89 us (12%)
  Pallas kernels  5.46 us (9%)
  waiting for transfers between devices  1.57 us (3%)
  between operations  0.69 us (1%)
    all_to_all x1, blocking collectives, body(): sums = lax.all_to_all(sums, 'space', 0, 0, axis_index_groups=[SPACE_ORDER])  19.8 us
    all_to_all x1, blocking collectives, body(): recv = lax.all_to_all(send, 'tm', 0, 0, axis_index_groups=[OUT_ORDER])  13 us
    all_to_all x1, blocking collectives, body(): back = lax.all_to_all(back, 'tm', 0, 0, axis_index_groups=[BACK_ORDER])  10.6 us
    ppermute x1, starting transfers between devices, body(): lax.ppermute(first, 'space', [((i + 1) % size, i) for i in range(size)])  6.89 us
    pallas_call x1, Pallas kernels, body(): call(inner_kernel, (one, four, two, two, feed), [VMEM] * 10, (VMEM,) * 5,...  2.79 us
    ppermute x1, waiting for transfers between devices, body(): lax.ppermute(last, 'space', [(i, (i + 1) % size) for i in range(size)])  1.56 us
  transfers between devices with their start and end apart: 2, of which 1 were waited for; matrix products, arithmetic and copies ran while one was open for 0% of the time, Pallas kernels for 5%

profile of v6, /device:TPU:1, one launch (start us, length us, event | category | flops | bytes accessed | tf_op | source)
XLA Modules:
  0.0 58.1 jit_solution(15678919809334539259)
XLA Ops:
  0.6 1.1 %edges.1 = (f32[112,256]{1,0:T(8,128)S(1)}, f32[112,256]{1,0:T(8,128)S(1)}) custom-call(f32[1,4,32,256]{3,2,1,0:T(8,128)} %lag.5, f32[1,2,4,32,256]{4,3,2,1,0:T(8,128)} %obs.5, f32[1,4,32,256]{3,2,1,0:T(8,128)} %inc.5, f32[4,32,256]{2,1,0:T(8,128)} %cx.3, f32[4,32,256]{2,1,0:T(8,128)} %cy.3, f32[4,32,256]{2,1,0:T(8,128)} %df.3), custom_call_target="tpu_custom_call" | custom-call | tf_op jit(solution)/shard_map/edges/pallas_call | solution.py:275
  1.8 6.9 %collective-permute-start = (f32[112,256]{1,0:T(8,128)S(1)}, f32[112,256]{1,0:T(8,128)S(1)}, u32[]{:S(2)}, u32[]{:S(2)}) collective-permute-start(f32[112,256]{1,0:T(8,128)S(1)} %get-tuple-element.15.first), channel_id=1, source_target_pairs={{1,0},{2,1},{3,2},{4,3},{5,4},{6,5},{7,6},{8,7},{9,8},{10,9},{11,1... | collective-permute-start | bytes 344072 | tf_op jit(solution)/shard_map/ppermute | solution.py:283
  8.6 0.0 collective-permute-start.1
  8.7 2.8 %inner_runs.1 = (f32[4,32,256]{2,1,0:T(8,128)S(1)}, f32[4,4,32,256]{3,2,1,0:T(8,128)S(1)}, f32[2,4,32,256]{3,2,1,0:T(8,128)S(1)}, f32[2,4,32,256]{3,2,1,0:T(8,128)S(1)}, f32[2,3,3,2,8,256]{5,4,3,2,1,0:T(8,128)S(1)}) custom-call(f32[1,4,32,256]{3,2,1,0:T(8,128)} %lag.5, f32[1,2,4,32,256]{4,3,2,1,0:T(8,128)} %obs.5, f32[1,4,32,256]{3,2,1,0:T(8,128)} %inc.5, ...), custom_call_target="tpu_custom_call" | custom-call | flops 8388608 | bytes 4194304 | tf_op jit(solution)/shard_map/inner_runs/pallas_call | solution.py:285
  11.5 0.0 collective-permute-done.nxt
  11.5 1.6 %collective-permute-done.1.prv = f32[112,256]{1,0:T(8,128)S(1)} collective-permute-done((f32[112,256]{1,0:T(8,128)S(1)}, f32[112,256]{1,0:T(8,128)S(1)}, u32[]{:S(2)}, u32[]{:S(2)}) %collective-permute-start.1) | collective-permute-done | bytes 114720 | tf_op jit(solution)/shard_map/ppermute | solution.py:284
  13.0 0.4 outer_runs.1
  13.5 13.0 %all_to_all.15.recv = f32[16,32,256]{2,1,0:T(8,128)S(1)} all-to-all(f32[16,32,256]{2,1,0:T(8,128)S(1)} %get-tuple-element.22), channel_id=1, replica_groups={{320,192,288,352,448,64,160,224,256,416,480,32,96,128,384,0},{321,193,2..., dimensions={0} | all-to-all | bytes 1048576 | tf_op jit(solution)/shard_map/all_to_all | solution.py:300
  26.5 0.2 window_sums.1
  26.7 19.8 %all_to_all.16.sums = f32[32,1,128]{2,1,0:T(1,128)S(1)} all-to-all(f32[32,1,128]{2,1,0:T(1,128)S(1)} %get-tuple-element.24), channel_id=1, replica_groups={{21,20,19,18,17,16,15,14,13,12,11,10,9,8,7,6,5,4,3,2,1,0,31,30,29,28,27..., dimensions={0} | all-to-all | bytes 32768 | tf_op jit(solution)/shard_map/all_to_all | solution.py:308
  46.6 0.0 copy-start
  46.6 0.0 copy-start.1
  46.6 0.0 copy-start.2
  46.6 10.6 %all_to_all.17.recv = f32[16,40,128]{2,1,0:T(8,128)S(1)} all-to-all(f32[16,40,128]{2,1,0:T(8,128)S(1)} %join.1), channel_id=1, replica_groups={{320,192,288,352,448,64,160,224,256,416,480,32,96,128,384,0},{321,193,2..., dimensions={0} | all-to-all | bytes 655360 | tf_op jit(solution)/shard_map/all_to_all | solution.py:316
  57.2 0.0 copy-done
  57.2 0.0 copy-done.1
  57.2 0.0 copy-done.2
  57.2 0.9 %update.1 = (f32[1,4,32,256]{3,2,1,0:T(8,128)}, f32[1,2,4,32,256]{4,3,2,1,0:T(8,128)}, f32[1,4,32,256]{3,2,1,0:T(8,128)}) custom-call(f32[16,40,128]{2,1,0:T(8,128)S(1)} %all_to_all.17.recv, f32[1,4,32,256]{3,2,1,0:T(8,128)S(1)} %copy-done.1, f32[1,2,4,32,256]{4,3,2,1,0:T(8,128)S(1)} %copy-done, f32[1,4,32,256]{3,2,1,0:T(8,128)S(1)} %copy-done.2, ...), custom_call_target="tpu_custom_call" | custom-call | tf_op jit(solution)/shard_map/update/pallas_call | solution.py:317
  (1 shorter events, 0.0 us)
Async XLA Ops:
  1.8 9.7 %collective-permute-start = (f32[112,256]{1,0:T(8,128)S(1)}, f32[112,256]{1,0:T(8,128)S(1)}, u32[]{:S(2)}, u32[]{:S(2)}) collective-permute-start(f32[112,256]{1,0:T(8,128)S(1)} %get-tuple-element.15.first), channel_id=1, source_target_pairs={{1,0},{2,1},{3,2},{4,3},{5,4},{6,5},{7,6},{8,7},{9,8},{10,9},{11,1... | collective-permute-start | bytes 344072 | tf_op jit(solution)/shard_map/ppermute | solution.py:283
  8.6 4.4 %collective-permute-start.1 = (f32[112,256]{1,0:T(8,128)S(1)}, f32[112,256]{1,0:T(8,128)S(1)}, u32[]{:S(2)}, u32[]{:S(2)}) collective-permute-start(f32[112,256]{1,0:T(8,128)S(1)} %get-tuple-element.16.last), channel_id=1, source_target_pairs={{0,1},{1,2},{2,3},{3,4},{4,5},{5,6},{6,7},{7,8},{8,9},{9,10},{10,1... | collective-permute-start | bytes 344072 | tf_op jit(solution)/shard_map/ppermute | solution.py:284
  46.6 10.6 %copy-start = (f32[1,2,4,32,256]{4,3,2,1,0:T(8,128)S(1)}, f32[1,2,4,32,256]{4,3,2,1,0:T(8,128)}, u32[]{:S(2)}) copy-start(f32[1,2,4,32,256]{4,3,2,1,0:T(8,128)} %obs.5) | copy-start | bytes 786436
  46.6 10.6 %copy-start.1 = (f32[1,4,32,256]{3,2,1,0:T(8,128)S(1)}, f32[1,4,32,256]{3,2,1,0:T(8,128)}, u32[]{:S(2)}) copy-start(f32[1,4,32,256]{3,2,1,0:T(8,128)} %lag.5) | copy-start | bytes 393220
  46.6 10.6 %copy-start.2 = (f32[1,4,32,256]{3,2,1,0:T(8,128)S(1)}, f32[1,4,32,256]{3,2,1,0:T(8,128)}, u32[]{:S(2)}) copy-start(f32[1,4,32,256]{3,2,1,0:T(8,128)} %inc.5) | copy-start | bytes 393220

commit v7 on v6

--- a/solution.py
+++ b/solution.py
@@ -38,6 +38,10 @@
     )
 
 
+def tile_of(f, m):
+    return 8 * (2 * f + m if f < 2 else 4 if f == 2 else 2 * f + m - 1)
+
+
 def edge_kernel(lag, obs, inc, cx, cy, df, first_out, last_out, first, last, sem):
     sources = [inc.at[0], obs.at[0, 1], obs.at[0, 0], lag.at[0], cx, cy, df]
     copies = []
@@ -48,10 +52,20 @@
         c.start()
     for c in copies:
         c.wait()
-    low = lax.broadcasted_iota(jnp.int32, (8, NY), 0) < 4
-    for f in range(EDGE):
+    row = lax.broadcasted_iota(jnp.int32, (8, NY), 0)
+    low = row < 4
+    two_first = two_last = jnp.zeros((8, NY), F32)
+    for l in range(LEV):
+        at = 4 * (l % 2) + 2 * (l // 2)
+        mine = (row >= at) & (row < at + 2)
+        two_first = jnp.where(mine, turn(first[2, l], at), two_first)
+        two_last = jnp.where(mine, turn(last[2, l], at - 6), two_last)
+    k = tile_of(2, 0)
+    first_out[k : k + 8, :] = two_first
+    last_out[k : k + 8, :] = two_last
+    for f in (0, 1, 3, 4, 5, 6):
         for m in range(2):
-            k = 8 * (2 * f + m)
+            k = tile_of(f, m)
             first_out[k : k + 8, :] = jnp.where(low, first[f, 2 * m], pltpu.roll(first[f, 2 * m + 1], 4, 0))
             last_out[k : k + 8, :] = jnp.where(low, pltpu.roll(last[f, 2 * m], 4, 0), last[f, 2 * m + 1])
 
@@ -122,7 +136,7 @@
     inward = 1 - 2 * side
 
     def tile(ref, f):
-        k = 8 * (2 * f + m)
+        k = tile_of(f, m)
         return ref[k : k + 8, :]
 
     def rows(f, s):
@@ -143,7 +157,9 @@
     for s in range(STEPS):
         if s == STEPS // 2:
             middle = q
-            p = p + moved(rows(2, 0), 2)
+            force = tile(nxt if side == 0 else prv, 2)
+            force = turn(force, 2 - 2 * m if side == 0 else -2 * m)
+            p = p + jnp.where(i >= 2 if side == 0 else i < 2, force, 0.0)
         there = weights(rows(4, s + 1), rows(5, s + 1), rows(6, s + 1))
         a0, ae, aw, an, as_ = there
         ahead, behind = (ae, aw) if side == 0 else (aw, ae)
@@ -268,7 +284,7 @@
 def body(lag, obs, inc, mside, oside, mvar, ovar, cx, cy, df):
     sds = jax.ShapeDtypeStruct
     size = lax.axis_size("space")
-    edge = sds((EDGE * LEV * 4, NY), F32)
+    edge = sds((tile_of(EDGE, 0), NY), F32)
     one, two, four = (sds(n + (LEV, ROWS, NY), F32) for n in ((), (2,), (4,)))
     feed = sds((2, 3, STEPS - 1, LEV // 2, 8, NY), F32)
     held = [pltpu.with_memory_space_constraint(x, pltpu.HBM) for x in (lag, obs, inc, mside, oside, mvar, ovar, cx, cy, df)]

time: 58.5 us -> 58.5 us (level)
  no operation moved by 1% of the time
where the time goes in v7:
time: 58.5 us; the launch traced here: 58.1 us
  blocking collectives  43.5 us (74%)
  starting transfers between devices  6.89 us (12%)
  Pallas kernels  5.46 us (9%)
  waiting for transfers between devices  1.56 us (3%)
  between operations  0.69 us (1%)
    all_to_all x1, blocking collectives, body(): sums = lax.all_to_all(sums, 'space', 0, 0, axis_index_groups=[SPACE_ORDER])  19.8 us
    all_to_all x1, blocking collectives, body(): recv = lax.all_to_all(send, 'tm', 0, 0, axis_index_groups=[OUT_ORDER])  13 us
    all_to_all x1, blocking collectives, body(): back = lax.all_to_all(back, 'tm', 0, 0, axis_index_groups=[BACK_ORDER])  10.6 us
    ppermute x1, starting transfers between devices, body(): lax.ppermute(first, 'space', [((i + 1) % size, i) for i in range(size)])  6.89 us
    pallas_call x1, Pallas kernels, body(): call(inner_kernel, (one, four, two, two, feed), [VMEM] * 10, (VMEM,) * 5,...  2.79 us
    ppermute x1, waiting for transfers between devices, body(): lax.ppermute(last, 'space', [(i, (i + 1) % size) for i in range(size)])  1.55 us
  transfers between devices with their start and end apart: 2, of which 1 were waited for; matrix products, arithmetic and copies ran while one was open for 0% of the time, Pallas kernels for 5%

profile of v7, /device:TPU:1, one launch (start us, length us, event | category | flops | bytes accessed | tf_op | source)
XLA Modules:
  0.0 58.1 jit_solution(10054301426446643443)
XLA Ops:
  0.6 1.1 %edges.1 = (f32[104,256]{1,0:T(8,128)S(1)}, f32[104,256]{1,0:T(8,128)S(1)}) custom-call(f32[1,4,32,256]{3,2,1,0:T(8,128)} %lag.5, f32[1,2,4,32,256]{4,3,2,1,0:T(8,128)} %obs.5, f32[1,4,32,256]{3,2,1,0:T(8,128)} %inc.5, f32[4,32,256]{2,1,0:T(8,128)} %cx.3, f32[4,32,256]{2,1,0:T(8,128)} %cy.3, f32[4,32,256]{2,1,0:T(8,128)} %df.3), custom_call_target="tpu_custom_call" | custom-call | tf_op jit(solution)/shard_map/edges/pallas_call | solution.py:291
  1.8 6.9 %collective-permute-start = (f32[104,256]{1,0:T(8,128)S(1)}, f32[104,256]{1,0:T(8,128)S(1)}, u32[]{:S(2)}, u32[]{:S(2)}) collective-permute-start(f32[104,256]{1,0:T(8,128)S(1)} %get-tuple-element.15.first), channel_id=1, source_target_pairs={{1,0},{2,1},{3,2},{4,3},{5,4},{6,5},{7,6},{8,7},{9,8},{10,9},{11,1... | collective-permute-start | bytes 319496 | tf_op jit(solution)/shard_map/ppermute | solution.py:299
  8.7 0.0 collective-permute-start.1
  8.7 2.8 %inner_runs.1 = (f32[4,32,256]{2,1,0:T(8,128)S(1)}, f32[4,4,32,256]{3,2,1,0:T(8,128)S(1)}, f32[2,4,32,256]{3,2,1,0:T(8,128)S(1)}, f32[2,4,32,256]{3,2,1,0:T(8,128)S(1)}, f32[2,3,3,2,8,256]{5,4,3,2,1,0:T(8,128)S(1)}) custom-call(f32[1,4,32,256]{3,2,1,0:T(8,128)} %lag.5, f32[1,2,4,32,256]{4,3,2,1,0:T(8,128)} %obs.5, f32[1,4,32,256]{3,2,1,0:T(8,128)} %inc.5, ...), custom_call_target="tpu_custom_call" | custom-call | flops 8388608 | bytes 4194304 | tf_op jit(solution)/shard_map/inner_runs/pallas_call | solution.py:301
  11.5 0.0 collective-permute-done.nxt
  11.5 1.6 %collective-permute-done.1.prv = f32[104,256]{1,0:T(8,128)S(1)} collective-permute-done((f32[104,256]{1,0:T(8,128)S(1)}, f32[104,256]{1,0:T(8,128)S(1)}, u32[]{:S(2)}, u32[]{:S(2)}) %collective-permute-start.1) | collective-permute-done | bytes 106528 | tf_op jit(solution)/shard_map/ppermute | solution.py:300
  13.0 0.4 outer_runs.1
  13.5 13.0 %all_to_all.15.recv = f32[16,32,256]{2,1,0:T(8,128)S(1)} all-to-all(f32[16,32,256]{2,1,0:T(8,128)S(1)} %get-tuple-element.22), channel_id=1, replica_groups={{320,192,288,352,448,64,160,224,256,416,480,32,96,128,384,0},{321,193,2..., dimensions={0} | all-to-all | bytes 1048576 | tf_op jit(solution)/shard_map/all_to_all | solution.py:316
  26.5 0.2 window_sums.1
  26.7 19.8 %all_to_all.16.sums = f32[32,1,128]{2,1,0:T(1,128)S(1)} all-to-all(f32[32,1,128]{2,1,0:T(1,128)S(1)} %get-tuple-element.24), channel_id=1, replica_groups={{21,20,19,18,17,16,15,14,13,12,11,10,9,8,7,6,5,4,3,2,1,0,31,30,29,28,27..., dimensions={0} | all-to-all | bytes 32768 | tf_op jit(solution)/shard_map/all_to_all | solution.py:324
  46.6 0.0 copy-start
  46.6 0.0 copy-start.1
  46.6 0.0 copy-start.2
  46.6 10.6 %all_to_all.17.recv = f32[16,40,128]{2,1,0:T(8,128)S(1)} all-to-all(f32[16,40,128]{2,1,0:T(8,128)S(1)} %join.1), channel_id=1, replica_groups={{320,192,288,352,448,64,160,224,256,416,480,32,96,128,384,0},{321,193,2..., dimensions={0} | all-to-all | bytes 655360 | tf_op jit(solution)/shard_map/all_to_all | solution.py:332
  57.2 0.0 copy-done
  57.2 0.0 copy-done.1
  57.2 0.0 copy-done.2
  57.2 0.9 %update.1 = (f32[1,4,32,256]{3,2,1,0:T(8,128)}, f32[1,2,4,32,256]{4,3,2,1,0:T(8,128)}, f32[1,4,32,256]{3,2,1,0:T(8,128)}) custom-call(f32[16,40,128]{2,1,0:T(8,128)S(1)} %all_to_all.17.recv, f32[1,4,32,256]{3,2,1,0:T(8,128)S(1)} %copy-done.1, f32[1,2,4,32,256]{4,3,2,1,0:T(8,128)S(1)} %copy-done, f32[1,4,32,256]{3,2,1,0:T(8,128)S(1)} %copy-done.2, ...), custom_call_target="tpu_custom_call" | custom-call | tf_op jit(solution)/shard_map/update/pallas_call | solution.py:333
  (1 shorter events, 0.0 us)
Async XLA Ops:
  1.8 9.7 %collective-permute-start = (f32[104,256]{1,0:T(8,128)S(1)}, f32[104,256]{1,0:T(8,128)S(1)}, u32[]{:S(2)}, u32[]{:S(2)}) collective-permute-start(f32[104,256]{1,0:T(8,128)S(1)} %get-tuple-element.15.first), channel_id=1, source_target_pairs={{1,0},{2,1},{3,2},{4,3},{5,4},{6,5},{7,6},{8,7},{9,8},{10,9},{11,1... | collective-permute-start | bytes 319496 | tf_op jit(solution)/shard_map/ppermute | solution.py:299
  8.7 4.4 %collective-permute-start.1 = (f32[104,256]{1,0:T(8,128)S(1)}, f32[104,256]{1,0:T(8,128)S(1)}, u32[]{:S(2)}, u32[]{:S(2)}) collective-permute-start(f32[104,256]{1,0:T(8,128)S(1)} %get-tuple-element.16.last), channel_id=1, source_target_pairs={{0,1},{1,2},{2,3},{3,4},{4,5},{5,6},{6,7},{7,8},{8,9},{9,10},{10,1... | collective-permute-start | bytes 319496 | tf_op jit(solution)/shard_map/ppermute | solution.py:300
  46.6 10.6 %copy-start = (f32[1,2,4,32,256]{4,3,2,1,0:T(8,128)S(1)}, f32[1,2,4,32,256]{4,3,2,1,0:T(8,128)}, u32[]{:S(2)}) copy-start(f32[1,2,4,32,256]{4,3,2,1,0:T(8,128)} %obs.5) | copy-start | bytes 786436
  46.6 10.6 %copy-start.1 = (f32[1,4,32,256]{3,2,1,0:T(8,128)S(1)}, f32[1,4,32,256]{3,2,1,0:T(8,128)}, u32[]{:S(2)}) copy-start(f32[1,4,32,256]{3,2,1,0:T(8,128)} %lag.5) | copy-start | bytes 393220
  46.6 10.6 %copy-start.2 = (f32[1,4,32,256]{3,2,1,0:T(8,128)S(1)}, f32[1,4,32,256]{3,2,1,0:T(8,128)}, u32[]{:S(2)}) copy-start(f32[1,4,32,256]{3,2,1,0:T(8,128)} %inc.5) | copy-start | bytes 393220

commit v8 on v6

--- a/solution.py
+++ b/solution.py
@@ -18,7 +18,7 @@
 
 SPACE_ORDER = [2 * (z % 16) + core for z in range(26, 10, -1) for core in (1, 0)]
 OUT_ORDER = [10, 6, 9, 11, 14, 2, 5, 7, 8, 13, 15, 1, 3, 4, 12, 0]
-BACK_ORDER = OUT_ORDER
+BACK_ORDER = OUT_ORDER[:1] + OUT_ORDER[:0:-1]
 OUT_AT = [OUT_ORDER.index(w) for w in range(NW)]
 BACK_AT = [BACK_ORDER.index(w) for w in range(NW)]
 

time: 58.5 us -> 58.4 us (level)
  no operation moved by 1% of the time
where the time goes in v8:
time: 58.4 us; the launch traced here: 57.8 us
  blocking collectives  43.2 us (74%)
  starting transfers between devices  6.89 us (12%)
  Pallas kernels  5.46 us (9%)
  waiting for transfers between devices  1.57 us (3%)
  between operations  0.69 us (1%)
    all_to_all x1, blocking collectives, body(): sums = lax.all_to_all(sums, 'space', 0, 0, axis_index_groups=[SPACE_ORDER])  19.8 us
    all_to_all x1, blocking collectives, body(): recv = lax.all_to_all(send, 'tm', 0, 0, axis_index_groups=[OUT_ORDER])  13 us
    all_to_all x1, blocking collectives, body(): back = lax.all_to_all(back, 'tm', 0, 0, axis_index_groups=[BACK_ORDER])  10.3 us
    ppermute x1, starting transfers between devices, body(): lax.ppermute(first, 'space', [((i + 1) % size, i) for i in range(size)])  6.89 us
    pallas_call x1, Pallas kernels, body(): call(inner_kernel, (one, four, two, two, feed), [VMEM] * 10, (VMEM,) * 5,...  2.79 us
    ppermute x1, waiting for transfers between devices, body(): lax.ppermute(last, 'space', [(i, (i + 1) % size) for i in range(size)])  1.56 us
  transfers between devices with their start and end apart: 2, of which 1 were waited for; matrix products, arithmetic and copies ran while one was open for 0% of the time, Pallas kernels for 5%

profile of v8, /device:TPU:1, one launch (start us, length us, event | category | flops | bytes accessed | tf_op | source)
XLA Modules:
  0.0 57.8 jit_solution(1989519677057435717)
XLA Ops:
  0.6 1.1 %edges.1 = (f32[112,256]{1,0:T(8,128)S(1)}, f32[112,256]{1,0:T(8,128)S(1)}) custom-call(f32[1,4,32,256]{3,2,1,0:T(8,128)} %lag.5, f32[1,2,4,32,256]{4,3,2,1,0:T(8,128)} %obs.5, f32[1,4,32,256]{3,2,1,0:T(8,128)} %inc.5, f32[4,32,256]{2,1,0:T(8,128)} %cx.3, f32[4,32,256]{2,1,0:T(8,128)} %cy.3, f32[4,32,256]{2,1,0:T(8,128)} %df.3), custom_call_target="tpu_custom_call" | custom-call | tf_op jit(solution)/shard_map/edges/pallas_call | solution.py:275
  1.8 6.9 %collective-permute-start = (f32[112,256]{1,0:T(8,128)S(1)}, f32[112,256]{1,0:T(8,128)S(1)}, u32[]{:S(2)}, u32[]{:S(2)}) collective-permute-start(f32[112,256]{1,0:T(8,128)S(1)} %get-tuple-element.15.first), channel_id=1, source_target_pairs={{1,0},{2,1},{3,2},{4,3},{5,4},{6,5},{7,6},{8,7},{9,8},{10,9},{11,1... | collective-permute-start | bytes 344072 | tf_op jit(solution)/shard_map/ppermute | solution.py:283
  8.6 0.0 collective-permute-start.1
  8.7 2.8 %inner_runs.1 = (f32[4,32,256]{2,1,0:T(8,128)S(1)}, f32[4,4,32,256]{3,2,1,0:T(8,128)S(1)}, f32[2,4,32,256]{3,2,1,0:T(8,128)S(1)}, f32[2,4,32,256]{3,2,1,0:T(8,128)S(1)}, f32[2,3,3,2,8,256]{5,4,3,2,1,0:T(8,128)S(1)}) custom-call(f32[1,4,32,256]{3,2,1,0:T(8,128)} %lag.5, f32[1,2,4,32,256]{4,3,2,1,0:T(8,128)} %obs.5, f32[1,4,32,256]{3,2,1,0:T(8,128)} %inc.5, ...), custom_call_target="tpu_custom_call" | custom-call | flops 8388608 | bytes 4194304 | tf_op jit(solution)/shard_map/inner_runs/pallas_call | solution.py:285
  11.5 0.0 collective-permute-done.nxt
  11.5 1.6 %collective-permute-done.1.prv = f32[112,256]{1,0:T(8,128)S(1)} collective-permute-done((f32[112,256]{1,0:T(8,128)S(1)}, f32[112,256]{1,0:T(8,128)S(1)}, u32[]{:S(2)}, u32[]{:S(2)}) %collective-permute-start.1) | collective-permute-done | bytes 114720 | tf_op jit(solution)/shard_map/ppermute | solution.py:284
  13.0 0.4 outer_runs.1
  13.5 13.0 %all_to_all.15.recv = f32[16,32,256]{2,1,0:T(8,128)S(1)} all-to-all(f32[16,32,256]{2,1,0:T(8,128)S(1)} %get-tuple-element.22), channel_id=1, replica_groups={{320,192,288,352,448,64,160,224,256,416,480,32,96,128,384,0},{321,193,2..., dimensions={0} | all-to-all | bytes 1048576 | tf_op jit(solution)/shard_map/all_to_all | solution.py:300
  26.5 0.2 window_sums.1
  26.7 19.8 %all_to_all.16.sums = f32[32,1,128]{2,1,0:T(1,128)S(1)} all-to-all(f32[32,1,128]{2,1,0:T(1,128)S(1)} %get-tuple-element.24), channel_id=1, replica_groups={{21,20,19,18,17,16,15,14,13,12,11,10,9,8,7,6,5,4,3,2,1,0,31,30,29,28,27..., dimensions={0} | all-to-all | bytes 32768 | tf_op jit(solution)/shard_map/all_to_all | solution.py:308
  46.6 0.0 copy-start
  46.6 0.0 copy-start.1
  46.6 0.0 copy-start.2
  46.6 10.3 %all_to_all.17.recv = f32[16,40,128]{2,1,0:T(8,128)S(1)} all-to-all(f32[16,40,128]{2,1,0:T(8,128)S(1)} %join.1), channel_id=1, replica_groups={{320,0,384,128,96,32,480,416,256,224,160,64,448,352,288,192},{321,1,385..., dimensions={0} | all-to-all | bytes 655360 | tf_op jit(solution)/shard_map/all_to_all | solution.py:316
  56.9 0.0 copy-done
  56.9 0.0 copy-done.1
  56.9 0.0 copy-done.2
  56.9 0.9 %update.1 = (f32[1,4,32,256]{3,2,1,0:T(8,128)}, f32[1,2,4,32,256]{4,3,2,1,0:T(8,128)}, f32[1,4,32,256]{3,2,1,0:T(8,128)}) custom-call(f32[16,40,128]{2,1,0:T(8,128)S(1)} %all_to_all.17.recv, f32[1,4,32,256]{3,2,1,0:T(8,128)S(1)} %copy-done.1, f32[1,2,4,32,256]{4,3,2,1,0:T(8,128)S(1)} %copy-done, f32[1,4,32,256]{3,2,1,0:T(8,128)S(1)} %copy-done.2, ...), custom_call_target="tpu_custom_call" | custom-call | tf_op jit(solution)/shard_map/update/pallas_call | solution.py:317
  (1 shorter events, 0.0 us)
Async XLA Ops:
  1.8 9.7 %collective-permute-start = (f32[112,256]{1,0:T(8,128)S(1)}, f32[112,256]{1,0:T(8,128)S(1)}, u32[]{:S(2)}, u32[]{:S(2)}) collective-permute-start(f32[112,256]{1,0:T(8,128)S(1)} %get-tuple-element.15.first), channel_id=1, source_target_pairs={{1,0},{2,1},{3,2},{4,3},{5,4},{6,5},{7,6},{8,7},{9,8},{10,9},{11,1... | collective-permute-start | bytes 344072 | tf_op jit(solution)/shard_map/ppermute | solution.py:283
  8.6 4.4 %collective-permute-start.1 = (f32[112,256]{1,0:T(8,128)S(1)}, f32[112,256]{1,0:T(8,128)S(1)}, u32[]{:S(2)}, u32[]{:S(2)}) collective-permute-start(f32[112,256]{1,0:T(8,128)S(1)} %get-tuple-element.16.last), channel_id=1, source_target_pairs={{0,1},{1,2},{2,3},{3,4},{4,5},{5,6},{6,7},{7,8},{8,9},{9,10},{10,1... | collective-permute-start | bytes 344072 | tf_op jit(solution)/shard_map/ppermute | solution.py:284
  46.6 10.3 %copy-start = (f32[1,2,4,32,256]{4,3,2,1,0:T(8,128)S(1)}, f32[1,2,4,32,256]{4,3,2,1,0:T(8,128)}, u32[]{:S(2)}) copy-start(f32[1,2,4,32,256]{4,3,2,1,0:T(8,128)} %obs.5) | copy-start | bytes 786436
  46.6 10.3 %copy-start.1 = (f32[1,4,32,256]{3,2,1,0:T(8,128)S(1)}, f32[1,4,32,256]{3,2,1,0:T(8,128)}, u32[]{:S(2)}) copy-start(f32[1,4,32,256]{3,2,1,0:T(8,128)} %lag.5) | copy-start | bytes 393220
  46.6 10.3 %copy-start.2 = (f32[1,4,32,256]{3,2,1,0:T(8,128)S(1)}, f32[1,4,32,256]{3,2,1,0:T(8,128)}, u32[]{:S(2)}) copy-start(f32[1,4,32,256]{3,2,1,0:T(8,128)} %inc.5) | copy-start | bytes 393220

commit v9 on v6

--- a/solution.py
+++ b/solution.py
@@ -280,8 +280,8 @@
         [pltpu.VMEM((EDGE, LEV, 8, NY), F32)] * 2 + [pltpu.SemaphoreType.DMA((2 * EDGE,))],
         name="edges",
     )(*held[:3], *held[7:])
+    prv = lax.ppermute(last, "space", [(i, (i + 1) % size) for i in range(size)])
     nxt = lax.ppermute(first, "space", [((i + 1) % size, i) for i in range(size)])
-    prv = lax.ppermute(last, "space", [(i, (i + 1) % size) for i in range(size)])
     inner = call(
         inner_kernel,
         (one, four, two, two, feed),

time: 58.5 us -> 58.5 us (level)
  no operation moved by 1% of the time
where the time goes in v9:
time: 58.5 us; the launch traced here: 58.1 us
  blocking collectives  43.5 us (74%)
  starting transfers between devices  6.89 us (12%)
  Pallas kernels  5.46 us (9%)
  waiting for transfers between devices  1.57 us (3%)
  between operations  0.69 us (1%)
    all_to_all x1, blocking collectives, body(): sums = lax.all_to_all(sums, 'space', 0, 0, axis_index_groups=[SPACE_ORDER])  19.8 us
    all_to_all x1, blocking collectives, body(): recv = lax.all_to_all(send, 'tm', 0, 0, axis_index_groups=[OUT_ORDER])  13 us
    all_to_all x1, blocking collectives, body(): back = lax.all_to_all(back, 'tm', 0, 0, axis_index_groups=[BACK_ORDER])  10.6 us
    ppermute x1, starting transfers between devices, body(): lax.ppermute(first, 'space', [((i + 1) % size, i) for i in range(size)])  6.89 us
    pallas_call x1, Pallas kernels, body(): call(inner_kernel, (one, four, two, two, feed), [VMEM] * 10, (VMEM,) * 5,...  2.79 us
    ppermute x1, waiting for transfers between devices, body(): lax.ppermute(last, 'space', [(i, (i + 1) % size) for i in range(size)])  1.56 us
  transfers between devices with their start and end apart: 2, of which 1 were waited for; matrix products, arithmetic and copies ran while one was open for 0% of the time, Pallas kernels for 5%

profile of v9, /device:TPU:1, one launch (start us, length us, event | category | flops | bytes accessed | tf_op | source)
XLA Modules:
  0.0 58.1 jit_solution(15678919809334539259)
XLA Ops:
  0.6 1.1 %edges.1 = (f32[112,256]{1,0:T(8,128)S(1)}, f32[112,256]{1,0:T(8,128)S(1)}) custom-call(f32[1,4,32,256]{3,2,1,0:T(8,128)} %lag.5, f32[1,2,4,32,256]{4,3,2,1,0:T(8,128)} %obs.5, f32[1,4,32,256]{3,2,1,0:T(8,128)} %inc.5, f32[4,32,256]{2,1,0:T(8,128)} %cx.3, f32[4,32,256]{2,1,0:T(8,128)} %cy.3, f32[4,32,256]{2,1,0:T(8,128)} %df.3), custom_call_target="tpu_custom_call" | custom-call | tf_op jit(solution)/shard_map/edges/pallas_call | solution.py:275
  1.8 6.9 %collective-permute-start = (f32[112,256]{1,0:T(8,128)S(1)}, f32[112,256]{1,0:T(8,128)S(1)}, u32[]{:S(2)}, u32[]{:S(2)}) collective-permute-start(f32[112,256]{1,0:T(8,128)S(1)} %get-tuple-element.15.first), channel_id=1, source_target_pairs={{1,0},{2,1},{3,2},{4,3},{5,4},{6,5},{7,6},{8,7},{9,8},{10,9},{11,1... | collective-permute-start | bytes 344072 | tf_op jit(solution)/shard_map/ppermute | solution.py:284
  8.6 0.0 collective-permute-start.1
  8.7 2.8 %inner_runs.1 = (f32[4,32,256]{2,1,0:T(8,128)S(1)}, f32[4,4,32,256]{3,2,1,0:T(8,128)S(1)}, f32[2,4,32,256]{3,2,1,0:T(8,128)S(1)}, f32[2,4,32,256]{3,2,1,0:T(8,128)S(1)}, f32[2,3,3,2,8,256]{5,4,3,2,1,0:T(8,128)S(1)}) custom-call(f32[1,4,32,256]{3,2,1,0:T(8,128)} %lag.5, f32[1,2,4,32,256]{4,3,2,1,0:T(8,128)} %obs.5, f32[1,4,32,256]{3,2,1,0:T(8,128)} %inc.5, ...), custom_call_target="tpu_custom_call" | custom-call | flops 8388608 | bytes 4194304 | tf_op jit(solution)/shard_map/inner_runs/pallas_call | solution.py:285
  11.5 0.0 collective-permute-done.nxt
  11.5 1.6 %collective-permute-done.1.prv = f32[112,256]{1,0:T(8,128)S(1)} collective-permute-done((f32[112,256]{1,0:T(8,128)S(1)}, f32[112,256]{1,0:T(8,128)S(1)}, u32[]{:S(2)}, u32[]{:S(2)}) %collective-permute-start.1) | collective-permute-done | bytes 114720 | tf_op jit(solution)/shard_map/ppermute | solution.py:283
  13.0 0.4 outer_runs.1
  13.5 13.0 %all_to_all.15.recv = f32[16,32,256]{2,1,0:T(8,128)S(1)} all-to-all(f32[16,32,256]{2,1,0:T(8,128)S(1)} %get-tuple-element.22), channel_id=1, replica_groups={{320,192,288,352,448,64,160,224,256,416,480,32,96,128,384,0},{321,193,2..., dimensions={0} | all-to-all | bytes 1048576 | tf_op jit(solution)/shard_map/all_to_all | solution.py:300
  26.5 0.2 window_sums.1
  26.7 19.8 %all_to_all.16.sums = f32[32,1,128]{2,1,0:T(1,128)S(1)} all-to-all(f32[32,1,128]{2,1,0:T(1,128)S(1)} %get-tuple-element.24), channel_id=1, replica_groups={{21,20,19,18,17,16,15,14,13,12,11,10,9,8,7,6,5,4,3,2,1,0,31,30,29,28,27..., dimensions={0} | all-to-all | bytes 32768 | tf_op jit(solution)/shard_map/all_to_all | solution.py:308
  46.6 0.0 copy-start
  46.6 0.0 copy-start.1
  46.6 0.0 copy-start.2
  46.6 10.6 %all_to_all.17.recv = f32[16,40,128]{2,1,0:T(8,128)S(1)} all-to-all(f32[16,40,128]{2,1,0:T(8,128)S(1)} %join.1), channel_id=1, replica_groups={{320,192,288,352,448,64,160,224,256,416,480,32,96,128,384,0},{321,193,2..., dimensions={0} | all-to-all | bytes 655360 | tf_op jit(solution)/shard_map/all_to_all | solution.py:316
  57.2 0.0 copy-done
  57.2 0.0 copy-done.1
  57.2 0.0 copy-done.2
  57.2 0.9 %update.1 = (f32[1,4,32,256]{3,2,1,0:T(8,128)}, f32[1,2,4,32,256]{4,3,2,1,0:T(8,128)}, f32[1,4,32,256]{3,2,1,0:T(8,128)}) custom-call(f32[16,40,128]{2,1,0:T(8,128)S(1)} %all_to_all.17.recv, f32[1,4,32,256]{3,2,1,0:T(8,128)S(1)} %copy-done.1, f32[1,2,4,32,256]{4,3,2,1,0:T(8,128)S(1)} %copy-done, f32[1,4,32,256]{3,2,1,0:T(8,128)S(1)} %copy-done.2, ...), custom_call_target="tpu_custom_call" | custom-call | tf_op jit(solution)/shard_map/update/pallas_call | solution.py:317
  (1 shorter events, 0.0 us)
Async XLA Ops:
  1.8 9.7 %collective-permute-start = (f32[112,256]{1,0:T(8,128)S(1)}, f32[112,256]{1,0:T(8,128)S(1)}, u32[]{:S(2)}, u32[]{:S(2)}) collective-permute-start(f32[112,256]{1,0:T(8,128)S(1)} %get-tuple-element.15.first), channel_id=1, source_target_pairs={{1,0},{2,1},{3,2},{4,3},{5,4},{6,5},{7,6},{8,7},{9,8},{10,9},{11,1... | collective-permute-start | bytes 344072 | tf_op jit(solution)/shard_map/ppermute | solution.py:284
  8.6 4.4 %collective-permute-start.1 = (f32[112,256]{1,0:T(8,128)S(1)}, f32[112,256]{1,0:T(8,128)S(1)}, u32[]{:S(2)}, u32[]{:S(2)}) collective-permute-start(f32[112,256]{1,0:T(8,128)S(1)} %get-tuple-element.16.last), channel_id=1, source_target_pairs={{0,1},{1,2},{2,3},{3,4},{4,5},{5,6},{6,7},{7,8},{8,9},{9,10},{10,1... | collective-permute-start | bytes 344072 | tf_op jit(solution)/shard_map/ppermute | solution.py:283
  46.6 10.6 %copy-start = (f32[1,2,4,32,256]{4,3,2,1,0:T(8,128)S(1)}, f32[1,2,4,32,256]{4,3,2,1,0:T(8,128)}, u32[]{:S(2)}) copy-start(f32[1,2,4,32,256]{4,3,2,1,0:T(8,128)} %obs.5) | copy-start | bytes 786436
  46.6 10.6 %copy-start.1 = (f32[1,4,32,256]{3,2,1,0:T(8,128)S(1)}, f32[1,4,32,256]{3,2,1,0:T(8,128)}, u32[]{:S(2)}) copy-start(f32[1,4,32,256]{3,2,1,0:T(8,128)} %lag.5) | copy-start | bytes 393220
  46.6 10.6 %copy-start.2 = (f32[1,4,32,256]{3,2,1,0:T(8,128)S(1)}, f32[1,4,32,256]{3,2,1,0:T(8,128)}, u32[]{:S(2)}) copy-start(f32[1,4,32,256]{3,2,1,0:T(8,128)} %inc.5) | copy-start | bytes 393220
